TPU v7x, 32 devices: a whole 2x2x4 slice. The times are simulated.
32 devices in a mesh: row: 8 (over z, x), col: 4 (over y, core).
Axes of the slice: x: 2, y: 2, z: 4, core: 2. Of those that a mesh axis runs over, the one named last changes fastest.
Arguments:
- inputs: bfloat16 [768, 8192], P('col', 'row'), may hold values from -6 to 6
- cotangent: bfloat16 [768, 8192], P('col', 'row'), may hold values from -6 to 6
- query_weight: bfloat16 [2, 768, 768], P(None, 'row', 'col'), may hold values from -0.21875 to 0.21875
- key_weight: bfloat16 [2, 768, 768], P(None, 'row', 'col'), may hold values from -0.21875 to 0.21875
- value_weight: bfloat16 [2, 768, 768], P(None, 'row', 'col'), may hold values from -0.21875 to 0.21875
- out_weight: bfloat16 [2, 768, 768], P(None, 'row', 'col'), may hold values from -1.75 to 1.75
- query_bias: bfloat16 [2, 4, 192], P(None, 'col', 'row'), may hold values from -4 to 4
- value_bias: bfloat16 [2, 4, 192], P(None, 'col', 'row'), may hold values from -1.5 to 1.5
- out_bias: bfloat16 [2, 4, 192], P(None, 'col', 'row'), may hold values from -4 to 4
- attention_gain: bfloat16 [2, 768], replicated, may hold values from 0.5 to 1.5
- attention_shift: bfloat16 [2, 768], replicated, may hold values from -4 to 4
- expand_weight: bfloat16 [2, 768, 3072], P(None, 'row', 'col'), may hold values from -0.21875 to 0.21875
- expand_bias: bfloat16 [2, 4, 768], P(None, 'col', 'row'), may hold values from -6 to 6
- contract_weight: bfloat16 [2, 768, 3072], P(None, 'row', 'col'), may hold values from -0.109375 to 0.109375
- contract_bias: bfloat16 [2, 4, 192], P(None, 'col', 'row'), may hold values from -4 to 4
- feed_gain: bfloat16 [2, 768], replicated, may hold values from 0.5 to 1.5
- feed_shift: bfloat16 [2, 768], replicated, may hold values from -4 to 4
Outputs:
- outputs: bfloat16 [768, 8192], P('col', 'row')
- inputs_grad: float32 [768, 8192], P('col', 'row')
- query_weight_grad: float32 [2, 768, 768], P(None, 'row', 'col')
- key_weight_grad: float32 [2, 768, 768], P(None, 'row', 'col')
- value_weight_grad: float32 [2, 768, 768], P(None, 'row', 'col')
- out_weight_grad: float32 [2, 768, 768], P(None, 'row', 'col')
- query_bias_grad: float32 [2, 4, 192], P(None, 'col', 'row')
- value_bias_grad: float32 [2, 4, 192], P(None, 'col', 'row')
- out_bias_grad: float32 [2, 4, 192], P(None, 'col', 'row')
- attention_gain_grad: float32 [2, 4, 192], P(None, 'col', 'row')
- attention_shift_grad: float32 [2, 4, 192], P(None, 'col', 'row')
- expand_weight_grad: float32 [2, 768, 3072], P(None, 'row', 'col')
- expand_bias_grad: float32 [2, 4, 768], P(None, 'col', 'row')
- contract_weight_grad: float32 [2, 768, 3072], P(None, 'row', 'col')
- contract_bias_grad: float32 [2, 4, 192], P(None, 'col', 'row')
- feed_gain_grad: float32 [2, 4, 192], P(None, 'col', 'row')
- feed_shift_grad: float32 [2, 4, 192], P(None, 'col', 'row')
All inputs are finite; a program needn't handle non-finite values.
Results may differ from a plain program's by a relative error of at most 0.023.
Values may be sent and summed in bfloat16 or wider, within the bound.
A program may use at most 192 MiB of HBM per device.

v0:
```python
import jax
import jax.numpy as jnp
from jax import lax
from jax.sharding import PartitionSpec as P

HD = 64
SEQ = 1024


EPSILON = 1e-05
NEG_FILL = -1e30


def contract_rows(left, right):
    return lax.dot_general(
        left, right, (((0,), (0,)), ((), ())), preferred_element_type=jnp.float32
    )


def contract_cols(left, right):
    return lax.dot_general(
        left, right, (((1,), (1,)), ((), ())), preferred_element_type=jnp.float32
    )


def gelu_tanh(values):
    return (
        0.5
        * values
        * (1.0 + jnp.tanh(0.7978845608028654 * (values + 0.044715 * values * values * values)))
    )


def col_sums(first, second):
    return lax.psum((first, second), "col")


def col_slice(whole, part_width, axis_dim):
    return lax.dynamic_slice_in_dim(whole, lax.axis_index("col") * part_width, part_width, axis_dim)


def norm_forward(resid_share, gain_full, shift_full):
    part_width = resid_share.shape[1]
    full_width = gain_full.shape[0]
    row_total, row_square = col_sums(
        jnp.sum(resid_share, axis=1), jnp.sum(resid_share * resid_share, axis=1)
    )
    row_mean = (row_total / full_width)[:, None]
    row_var = (row_square / full_width)[:, None] - row_mean * row_mean
    inv_std = lax.rsqrt(row_var + EPSILON)
    unit_rows = (resid_share - row_mean) * inv_std
    local_norm = unit_rows * col_slice(gain_full, part_width, 0) + col_slice(
        shift_full, part_width, 0
    )
    normed = lax.all_gather(local_norm.astype(jnp.bfloat16), "col", axis=1, tiled=True)
    return (normed, unit_rows, inv_std)


def branch_join(partial_rows, bias_share, resid_share, full_rows):
    part_width = resid_share.shape[1]
    bias_row = lax.dynamic_update_slice_in_dim(
        jnp.zeros((partial_rows.shape[1],), jnp.float32),
        bias_share.astype(jnp.float32),
        lax.axis_index("col") * part_width,
        0,
    )
    partial_rows = partial_rows + bias_row[None, :]
    resid_share = resid_share + lax.psum_scatter(
        partial_rows.astype(jnp.bfloat16), "col", scatter_dimension=1, tiled=True
    ).astype(jnp.float32)
    return (resid_share, full_rows)


def spread_grad(resid_grad):
    grad_low = resid_grad.astype(jnp.bfloat16)
    return (
        lax.all_gather(grad_low, "col", axis=1, tiled=True),
        jnp.sum(grad_low.astype(jnp.float32), axis=0),
    )


def norm_back(feature_part, unit_rows, inv_std, gain_full):
    normed_grad = lax.psum_scatter(
        feature_part.astype(jnp.bfloat16), "col", scatter_dimension=1, tiled=True
    ).astype(jnp.float32)
    part_width = unit_rows.shape[1]
    full_width = part_width * lax.axis_size("col")
    scaled = normed_grad * col_slice(gain_full, part_width, 0)
    first, second = col_sums(jnp.sum(scaled, axis=1), jnp.sum(scaled * unit_rows, axis=1))
    back_rows = inv_std * (
        scaled - first[:, None] / full_width - unit_rows * (second[:, None] / full_width)
    )
    return (back_rows, jnp.sum(normed_grad * unit_rows, axis=0), jnp.sum(normed_grad, axis=0))


def split_heads(rows_in):
    return rows_in.reshape(rows_in.shape[0] // SEQ, SEQ, rows_in.shape[1] // HD, HD)


def causal_scores(query_block, key_block, row_begin):
    scores = (
        jnp.einsum("sqhd,skhd->shqk", query_block, key_block, preferred_element_type=jnp.float32)
        * 0.125
    )
    grid_shape = (query_block.shape[1], key_block.shape[1])
    row_ids = row_begin + lax.broadcasted_iota(jnp.int32, grid_shape, 0)
    col_ids = lax.broadcasted_iota(jnp.int32, grid_shape, 1)
    return jnp.where((row_ids >= col_ids)[None, None], scores, NEG_FILL)


def attend(query_rows, key_rows, value_rows):
    block_rows = min(512, SEQ)
    query_seq = split_heads(query_rows)
    key_seq = split_heads(key_rows)
    value_seq = split_heads(value_rows)
    out_blocks = []
    log_totals = []
    for row_begin in range(0, SEQ, block_rows):
        row_end = row_begin + block_rows
        scores = causal_scores(query_seq[:, row_begin:row_end], key_seq[:, :row_end], row_begin)
        row_top = jnp.max(scores, axis=-1, keepdims=True)
        weights = jnp.exp(scores - row_top)
        row_total = jnp.sum(weights, axis=-1, keepdims=True)
        prob_rows = (weights / row_total).astype(jnp.bfloat16)
        out_blocks.append(
            jnp.einsum(
                "shqk,skhd->sqhd",
                prob_rows,
                value_seq[:, :row_end],
                preferred_element_type=jnp.float32,
            )
        )
        log_totals.append(row_top + jnp.log(row_total))
    mixed_rows = jnp.concatenate(out_blocks, axis=1).reshape(query_rows.shape).astype(jnp.bfloat16)
    return (mixed_rows, log_totals)


def attend_back(query_rows, key_rows, value_rows, log_totals, d_mixed):
    block_rows = min(512, SEQ)
    query_seq = split_heads(query_rows)
    key_seq = split_heads(key_rows)
    value_seq = split_heads(value_rows)
    grad_seq = split_heads(d_mixed)
    d_query_blocks = []
    d_key_seq = jnp.zeros(key_seq.shape, jnp.float32)
    d_value_seq = jnp.zeros(value_seq.shape, jnp.float32)
    for block_idx, row_begin in enumerate(range(0, SEQ, block_rows)):
        row_end = row_begin + block_rows
        tail_pad = ((0, 0), (0, SEQ - row_end), (0, 0), (0, 0))
        scores = causal_scores(query_seq[:, row_begin:row_end], key_seq[:, :row_end], row_begin)
        prob_rows = jnp.exp(scores - log_totals[block_idx])
        grad_block = grad_seq[:, row_begin:row_end]
        d_probs = jnp.einsum(
            "sqhd,skhd->shqk",
            grad_block,
            value_seq[:, :row_end],
            preferred_element_type=jnp.float32,
        )
        d_value_seq = d_value_seq + jnp.pad(
            jnp.einsum(
                "shqk,sqhd->skhd",
                prob_rows.astype(jnp.bfloat16),
                grad_block,
                preferred_element_type=jnp.float32,
            ),
            tail_pad,
        )
        inner_sum = jnp.sum(d_probs * prob_rows, axis=-1, keepdims=True)
        d_scores = (prob_rows * (d_probs - inner_sum)).astype(jnp.bfloat16)
        d_query_blocks.append(
            jnp.einsum(
                "shqk,skhd->sqhd",
                d_scores,
                key_seq[:, :row_end],
                preferred_element_type=jnp.float32,
            )
            * 0.125
        )
        d_key_seq = d_key_seq + jnp.pad(
            jnp.einsum(
                "shqk,sqhd->skhd",
                d_scores,
                query_seq[:, row_begin:row_end],
                preferred_element_type=jnp.float32,
            )
            * 0.125,
            tail_pad,
        )
    rows_shape = query_rows.shape
    d_query = jnp.concatenate(d_query_blocks, axis=1).reshape(rows_shape).astype(jnp.bfloat16)
    return (
        d_query,
        d_key_seq.reshape(rows_shape).astype(jnp.bfloat16),
        d_value_seq.reshape(rows_shape).astype(jnp.bfloat16),
    )


def stacked(groups, member, as_row):
    pieces = [group_item[member] for group_item in groups]
    if as_row:
        pieces = [piece_item.reshape(1, -1) for piece_item in pieces]
    return jnp.stack(pieces)


def local(
    inputs,
    cotangent,
    query_weight,
    key_weight,
    value_weight,
    out_weight,
    query_bias,
    value_bias,
    out_bias,
    attention_gain,
    attention_shift,
    expand_weight,
    expand_bias,
    contract_weight,
    contract_bias,
    feed_gain,
    feed_shift,
):
    layer_count = query_weight.shape[0]
    resid_share = inputs.astype(jnp.float32).T
    full_rows = None
    saved = []
    for layer_idx in range(layer_count):
        attn_parts = (
            lax.all_gather(query_weight[layer_idx], "row", axis=0, tiled=True),
            lax.all_gather(key_weight[layer_idx], "row", axis=0, tiled=True),
            lax.all_gather(value_weight[layer_idx], "row", axis=0, tiled=True),
            lax.all_gather(out_weight[layer_idx], "row", axis=0, tiled=True),
            lax.all_gather(query_bias[layer_idx].reshape(-1), "row", axis=0, tiled=True),
            lax.all_gather(value_bias[layer_idx].reshape(-1), "row", axis=0, tiled=True),
            lax.all_gather(out_bias[layer_idx].reshape(-1), "row", axis=0, tiled=True),
        )
        w_query, w_key, w_value, w_out, b_query, b_value, b_out = attn_parts
        gain_one = attention_gain[layer_idx].astype(jnp.float32)
        shift_one = attention_shift[layer_idx].astype(jnp.float32)
        norm_one, unit_one, inv_one = norm_forward(resid_share, gain_one, shift_one)
        query_rows = (
            jnp.dot(norm_one, w_query, preferred_element_type=jnp.float32) + b_query
        ).astype(jnp.bfloat16)
        key_rows = jnp.dot(norm_one, w_key, preferred_element_type=jnp.float32).astype(jnp.bfloat16)
        value_rows = (
            jnp.dot(norm_one, w_value, preferred_element_type=jnp.float32) + b_value
        ).astype(jnp.bfloat16)
        mixed_rows, log_totals = attend(query_rows, key_rows, value_rows)
        resid_share, full_rows = branch_join(
            contract_cols(mixed_rows, w_out), b_out, resid_share, full_rows
        )
        feed_parts = (
            lax.all_gather(expand_weight[layer_idx], "row", axis=0, tiled=True),
            lax.all_gather(contract_weight[layer_idx], "row", axis=0, tiled=True),
            lax.all_gather(expand_bias[layer_idx].reshape(-1), "row", axis=0, tiled=True),
            lax.all_gather(contract_bias[layer_idx].reshape(-1), "row", axis=0, tiled=True),
        )
        w_expand, w_contract, b_expand, b_contract = feed_parts
        gain_two = feed_gain[layer_idx].astype(jnp.float32)
        shift_two = feed_shift[layer_idx].astype(jnp.float32)
        norm_two, unit_two, inv_two = norm_forward(resid_share, gain_two, shift_two)
        before_act = jnp.dot(norm_two, w_expand, preferred_element_type=jnp.float32) + b_expand
        hidden_rows = gelu_tanh(before_act).astype(jnp.bfloat16)
        resid_share, full_rows = branch_join(
            contract_cols(hidden_rows, w_contract), b_contract, resid_share, full_rows
        )
        saved.append(
            (
                attn_parts,
                feed_parts,
                gain_one,
                gain_two,
                norm_one,
                unit_one,
                inv_one,
                query_rows,
                key_rows,
                value_rows,
                mixed_rows,
                log_totals,
                norm_two,
                unit_two,
                inv_two,
                before_act,
                hidden_rows,
            )
        )
    outputs = resid_share.astype(jnp.bfloat16).T
    resid_grad = cotangent.astype(jnp.float32).T
    attn_grads = [None] * layer_count
    feed_grads = [None] * layer_count
    for layer_idx in reversed(range(layer_count)):
        (
            attn_parts,
            feed_parts,
            gain_one,
            gain_two,
            norm_one,
            unit_one,
            inv_one,
            query_rows,
            key_rows,
            value_rows,
            mixed_rows,
            log_totals,
            norm_two,
            unit_two,
            inv_two,
            before_act,
            hidden_rows,
        ) = saved[layer_idx]
        w_query, w_key, w_value, w_out, b_query, b_value, b_out = attn_parts
        w_expand, w_contract, b_expand, b_contract = feed_parts
        branch_full, branch_total = spread_grad(resid_grad)
        d_hidden = jnp.dot(branch_full, w_contract, preferred_element_type=jnp.float32)
        d_before = jax.vjp(gelu_tanh, before_act)[1](d_hidden)[0].astype(jnp.bfloat16)
        contract_part = contract_rows(branch_full, hidden_rows)
        expand_part = contract_rows(norm_two, d_before)
        expand_bias_part = jnp.sum(d_before.astype(jnp.float32), axis=0)
        back_rows, gain_part, shift_part = norm_back(
            contract_cols(d_before, w_expand), unit_two, inv_two, gain_two
        )
        feed_grads[layer_idx] = (
            lax.psum_scatter(expand_part, "row", scatter_dimension=0, tiled=True),
            lax.psum_scatter(contract_part, "row", scatter_dimension=0, tiled=True),
            lax.psum_scatter(expand_bias_part, "row", scatter_dimension=0, tiled=True),
            lax.psum_scatter(branch_total, "row", scatter_dimension=0, tiled=True),
            lax.psum_scatter(gain_part, "row", scatter_dimension=0, tiled=True),
            lax.psum_scatter(shift_part, "row", scatter_dimension=0, tiled=True),
        )
        resid_grad = resid_grad + back_rows
        branch_full, branch_total = spread_grad(resid_grad)
        d_mixed = jnp.dot(branch_full, w_out, preferred_element_type=jnp.float32).astype(
            jnp.bfloat16
        )
        out_part = contract_rows(branch_full, mixed_rows)
        d_query, d_key, d_value = attend_back(query_rows, key_rows, value_rows, log_totals, d_mixed)
        feature_part = (
            contract_cols(d_query, w_query)
            + contract_cols(d_key, w_key)
            + contract_cols(d_value, w_value)
        )
        back_rows, gain_part, shift_part = norm_back(feature_part, unit_one, inv_one, gain_one)
        attn_grads[layer_idx] = (
            lax.psum_scatter(
                contract_rows(norm_one, d_query), "row", scatter_dimension=0, tiled=True
            ),
            lax.psum_scatter(
                contract_rows(norm_one, d_key), "row", scatter_dimension=0, tiled=True
            ),
            lax.psum_scatter(
                contract_rows(norm_one, d_value), "row", scatter_dimension=0, tiled=True
            ),
            lax.psum_scatter(out_part, "row", scatter_dimension=0, tiled=True),
            lax.psum_scatter(
                jnp.sum(d_query.astype(jnp.float32), axis=0), "row", scatter_dimension=0, tiled=True
            ),
            lax.psum_scatter(
                jnp.sum(d_value.astype(jnp.float32), axis=0), "row", scatter_dimension=0, tiled=True
            ),
            lax.psum_scatter(branch_total, "row", scatter_dimension=0, tiled=True),
            lax.psum_scatter(gain_part, "row", scatter_dimension=0, tiled=True),
            lax.psum_scatter(shift_part, "row", scatter_dimension=0, tiled=True),
        )
        resid_grad = resid_grad + back_rows
    return (
        outputs,
        resid_grad.T,
        stacked(attn_grads, 0, False),
        stacked(attn_grads, 1, False),
        stacked(attn_grads, 2, False),
        stacked(attn_grads, 3, False),
        stacked(attn_grads, 4, True),
        stacked(attn_grads, 5, True),
        stacked(attn_grads, 6, True),
        stacked(attn_grads, 7, True),
        stacked(attn_grads, 8, True),
        stacked(feed_grads, 0, False),
        stacked(feed_grads, 2, True),
        stacked(feed_grads, 1, False),
        stacked(feed_grads, 3, True),
        stacked(feed_grads, 4, True),
        stacked(feed_grads, 5, True),
    )


def solution(mesh):
    placed = (
        P("col", "row"),
        P("col", "row"),
        P(None, "row", "col"),
        P(None, "row", "col"),
        P(None, "row", "col"),
        P(None, "row", "col"),
        P(None, "col", "row"),
        P(None, "col", "row"),
        P(None, "col", "row"),
        P(),
        P(),
        P(None, "row", "col"),
        P(None, "col", "row"),
        P(None, "row", "col"),
        P(None, "col", "row"),
        P(),
        P(),
    )
    return jax.shard_map(
        local,
        mesh=mesh,
        in_specs=placed,
        out_specs=(
            P("col", "row"),
            P("col", "row"),
            P(None, "row", "col"),
            P(None, "row", "col"),
            P(None, "row", "col"),
            P(None, "row", "col"),
            P(None, "col", "row"),
            P(None, "col", "row"),
            P(None, "col", "row"),
            P(None, "col", "row"),
            P(None, "col", "row"),
            P(None, "row", "col"),
            P(None, "col", "row"),
            P(None, "row", "col"),
            P(None, "col", "row"),
            P(None, "col", "row"),
            P(None, "col", "row"),
        ),
        check_vma=False,
    )
```

profile of v0, /device:TPU:11, one launch (start us, length us, event | category | flops | bytes accessed | tf_op | source)
XLA Modules:
  0.0 1777.9 jit_solution(3949806545368616936)
XLA Ops:
  12.6 5.7 all-reduce.40
  29.0 12.7 all-reduce.41
  43.9 27.0 %all-gather.5 = bf16[1,768,192]{2,1,0:T(8,128)(2,1)} all-gather(bf16[1,96,192]{2,1,0:T(8,128)(2,1)S(1)} %get-tuple-element.103), channel_id=7, replica_groups=mesh['row'=8,'col'=4] {'row'}, dimensions={1}, use_global_device_ids=true | all-gather | bytes 331776 | tf_op jit(solution)/shard_map/all_gather | solution.py:233
  71.5 27.1 %all-gather = bf16[1,768,192]{2,1,0:T(8,128)(2,1)} all-gather(bf16[1,96,192]{2,1,0:T(8,128)(2,1)S(1)} %get-tuple-element.109), channel_id=2, replica_groups=mesh['row'=8,'col'=4] {'row'}, dimensions={1}, use_global_device_ids=true | all-gather | bytes 331776 | tf_op jit(solution)/shard_map/all_gather | solution.py:232
  99.2 24.7 %all-gather.4 = bf16[1,768,192]{2,1,0:T(8,128)(2,1)S(1)} all-gather(bf16[1,96,192]{2,1,0:T(8,128)(2,1)S(1)} %get-tuple-element.107), channel_id=6, replica_groups=mesh['row'=8,'col'=4] {'row'}, dimensions={1}, use_global_device_ids=true | all-gather | bytes 331776 | tf_op jit(solution)/shard_map/all_gather | solution.py:231
  124.5 24.6 %all-gather.2 = bf16[1,768,192]{2,1,0:T(8,128)(2,1)S(1)} all-gather(bf16[1,96,192]{2,1,0:T(8,128)(2,1)S(1)} %get-tuple-element.105), channel_id=4, replica_groups=mesh['row'=8,'col'=4] {'row'}, dimensions={1}, use_global_device_ids=true | all-gather | bytes 331776 | tf_op jit(solution)/shard_map/all_gather | solution.py:230
  171.3 57.0 %reduce-scatter.21.cloned.1.call-done = bf16[1024,192]{0,1:T(8,128)(2,1)} async-done(((bf16[1024,768]{0,1:T(8,128)(2,1)}), bf16[1024,192]{0,1:T(8,128)(2,1)}) %reduce-scatter.21.cloned.1.call-update) | async-done | bytes 393232 | tf_op jit(solution)/shard_map/reduce_scatter | solution.py:68
  229.5 6.4 all-reduce.39
  242.5 22.9 %all-gather.37.cloned.1.call-done = bf16[1024,768]{0,1:T(8,128)(2,1)} async-done(((bf16[1024,192]{0,1:T(8,128)(2,1)}), bf16[1024,768]{0,1:T(8,128)(2,1)}) %all-gather.37.cloned.1.call-update) | async-done | bytes 1572880 | tf_op jit(solution)/shard_map/all_gather | solution.py:55
  265.4 4.8 fusion.90
  270.3 36.5 %all-gather.53.cloned.1.call-done = bf16[1,768,768]{2,1,0:T(8,128)(2,1)} async-done(((bf16[1,96,768]{2,1,0:T(8,128)(2,1)}), bf16[1,768,768]{2,1,0:T(8,128)(2,1)}) %all-gather.53.cloned.1.call-update) | async-done | bytes 1179664 | tf_op jit(solution)/shard_map/all_gather | solution.py:255
  306.8 5.0 add_convert_fusion.4
  312.7 28.6 %reduce-scatter.23.cloned.1.call-done = bf16[1024,192]{0,1:T(8,128)(2,1)} async-done(((bf16[1024,768]{0,1:T(8,128)(2,1)}), bf16[1024,192]{0,1:T(8,128)(2,1)}) %reduce-scatter.23.cloned.1.call-update) | async-done | bytes 393232 | tf_op jit(solution)/shard_map/reduce_scatter | solution.py:68
  343.5 6.5 all-reduce.38
  354.8 24.5 %all-gather.16 = bf16[1,768,192]{2,1,0:T(8,128)(2,1)} all-gather(bf16[1,96,192]{2,1,0:T(8,128)(2,1)} %get-tuple-element.102), channel_id=18, replica_groups=mesh['row'=8,'col'=4] {'row'}, dimensions={1}, use_global_device_ids=true | all-gather | bytes 331776 | tf_op jit(solution)/shard_map/all_gather | solution.py:233
  379.3 26.8 %all-gather.11 = bf16[1,768,192]{2,1,0:T(8,128)(2,1)} all-gather(bf16[1,96,192]{2,1,0:T(8,128)(2,1)} %get-tuple-element.108), channel_id=13, replica_groups=mesh['row'=8,'col'=4] {'row'}, dimensions={1}, use_global_device_ids=true | all-gather | bytes 331776 | tf_op jit(solution)/shard_map/all_gather | solution.py:232
  406.1 27.5 %all-gather.15 = bf16[1,768,192]{2,1,0:T(8,128)(2,1)} all-gather(bf16[1,96,192]{2,1,0:T(8,128)(2,1)} %get-tuple-element.106), channel_id=17, replica_groups=mesh['row'=8,'col'=4] {'row'}, dimensions={1}, use_global_device_ids=true | all-gather | bytes 331776 | tf_op jit(solution)/shard_map/all_gather | solution.py:231
  433.6 27.5 %all-gather.13 = bf16[1,768,192]{2,1,0:T(8,128)(2,1)} all-gather(bf16[1,96,192]{2,1,0:T(8,128)(2,1)} %get-tuple-element.104), channel_id=15, replica_groups=mesh['row'=8,'col'=4] {'row'}, dimensions={1}, use_global_device_ids=true | all-gather | bytes 331776 | tf_op jit(solution)/shard_map/all_gather | solution.py:230
  480.6 54.4 %reduce-scatter.25.cloned.1.call-done = bf16[1024,192]{0,1:T(8,128)(2,1)} async-done(((bf16[1024,768]{0,1:T(8,128)(2,1)}), bf16[1024,192]{0,1:T(8,128)(2,1)}) %reduce-scatter.25.cloned.1.call-update) | async-done | bytes 393232 | tf_op jit(solution)/shard_map/reduce_scatter | solution.py:68
  537.3 6.4 all-reduce.37
  549.3 23.3 %all-gather.41.cloned.1.call-done = bf16[1024,768]{0,1:T(8,128)(2,1)} async-done(((bf16[1024,192]{0,1:T(8,128)(2,1)}), bf16[1024,768]{0,1:T(8,128)(2,1)}) %all-gather.41.cloned.1.call-update) | async-done | bytes 1572880 | tf_op jit(solution)/shard_map/all_gather | solution.py:55
  572.6 4.8 fusion.82
  577.5 36.5 %all-gather.57.cloned.1.call-done = bf16[1,768,768]{2,1,0:T(8,128)(2,1)} async-done(((bf16[1,96,768]{2,1,0:T(8,128)(2,1)}), bf16[1,768,768]{2,1,0:T(8,128)(2,1)}) %all-gather.57.cloned.1.call-update) | async-done | bytes 1179664 | tf_op jit(solution)/shard_map/all_gather | solution.py:255
  614.0 22.6 %all-gather.43.cloned.1.call-done = bf16[1024,768]{0,1:T(8,128)(2,1)} async-done(((bf16[1024,192]{0,1:T(8,128)(2,1)}), bf16[1024,768]{0,1:T(8,128)(2,1)}) %all-gather.43.cloned.1.call-update) | async-done | bytes 1572880 | tf_op jit(solution)/shard_map/all_gather | solution.py:77
  636.6 7.2 convert_reduce_fusion
  647.6 27.9 %reduce-scatter.29.cloned.1.call-done = bf16[1024,192]{0,1:T(8,128)(2,1)} async-done(((bf16[1024,768]{0,1:T(8,128)(2,1)}), bf16[1024,192]{0,1:T(8,128)(2,1)}) %reduce-scatter.29.cloned.1.call-update) | async-done | bytes 393232 | tf_op jit(solution)/shard_map/reduce_scatter | solution.py:83
  677.8 6.5 all-reduce.36
  685.0 3.1 convert_reduce_fusion.9
  690.0 19.5 %all-gather.45.cloned.1.call-done = bf16[1024,768]{0,1:T(8,128)(2,1)} async-done(((bf16[1024,192]{0,1:T(8,128)(2,1)}), bf16[1024,768]{0,1:T(8,128)(2,1)}) %all-gather.45.cloned.1.call-update) | async-done | bytes 1572880 | tf_op jit(solution)/shard_map/all_gather | solution.py:77
  729.7 4.9 add_convert_fusion.2
  734.7 22.7 %reduce-scatter.31.cloned.1.call-done = bf16[1024,192]{0,1:T(8,128)(2,1)} async-done(((bf16[1024,768]{0,1:T(8,128)(2,1)}), bf16[1024,192]{0,1:T(8,128)(2,1)}) %reduce-scatter.31.cloned.1.call-update) | async-done | bytes 393232 | tf_op jit(solution)/shard_map/reduce_scatter | solution.py:83
  759.6 6.5 all-reduce.35
  768.7 19.6 %reduce-scatter.27.cloned.1.call-done = bf16[1024,192]{0,1:T(8,128)(2,1)} async-done(((bf16[1024,768]{0,1:T(8,128)(2,1)}), bf16[1024,192]{0,1:T(8,128)(2,1)}) %reduce-scatter.27.cloned.1.call-update) | async-done | bytes 393232 | tf_op jit(solution)/shard_map/reduce_scatter | solution.py:68
  788.3 4.3 convert_reduce_fusion.8
  792.9 19.8 %all-gather.47.cloned.1.call-done = bf16[1024,768]{0,1:T(8,128)(2,1)} async-done(((bf16[1024,192]{0,1:T(8,128)(2,1)}), bf16[1024,768]{0,1:T(8,128)(2,1)}) %all-gather.47.cloned.1.call-update) | async-done | bytes 1572880 | tf_op jit(solution)/shard_map/all_gather | solution.py:77
  812.7 7.2 convert_reduce_fusion.1
  823.7 27.6 %reduce-scatter.33.cloned.1.call-done = bf16[1024,192]{0,1:T(8,128)(2,1)} async-done(((bf16[1024,768]{0,1:T(8,128)(2,1)}), bf16[1024,192]{0,1:T(8,128)(2,1)}) %reduce-scatter.33.cloned.1.call-update) | async-done | bytes 393232 | tf_op jit(solution)/shard_map/reduce_scatter | solution.py:83
  853.5 6.5 all-reduce.34
  861.5 3.1 convert_reduce_fusion.10
  864.6 5.4 convolution_bitcast_fusion
  870.1 5.4 fusion.177
  875.6 4.8 fusion.207
  880.4 4.7 fusion.206
  885.4 3.0 fusion.205
  888.5 3.0 fusion.204
  893.0 3.0 fusion.203
  898.9 4.7 convert_reduce_fusion.12
  905.9 3.0 fusion.201
  911.0 4.0 multiply_reduce_fusion
  935.6 20.3 %reduce-scatter.59.cloned.1.call-done = f32[96,768]{1,0:T(8,128)} async-done(((f32[768,768]{1,0:T(8,128)}), f32[96,768]{1,0:T(8,128)}) %reduce-scatter.59.cloned.1.call-update) | async-done | bytes 294928 | tf_op jit(solution)/shard_map/reduce_scatter | solution.py:326
  955.9 71.8 %reduce-scatter.57.cloned.1.call-done = f32[96,768]{1,0:T(8,128)} async-done(((f32[768,768]{1,0:T(8,128)}), f32[96,768]{1,0:T(8,128)}) %reduce-scatter.57.cloned.1.call-update) | async-done | bytes 294928 | tf_op jit(solution)/shard_map/reduce_scatter | solution.py:326
  1029.6 70.0 %reduce-scatter.55.cloned.1.call-done = f32[96,768]{1,0:T(8,128)} async-done(((f32[768,768]{1,0:T(8,128)}), f32[96,768]{1,0:T(8,128)}) %reduce-scatter.55.cloned.1.call-update) | async-done | bytes 294928 | tf_op jit(solution)/shard_map/reduce_scatter | solution.py:325
  1099.6 71.9 %reduce-scatter.53.cloned.1.call-done = f32[96,768]{1,0:T(8,128)} async-done(((f32[768,768]{1,0:T(8,128)}), f32[96,768]{1,0:T(8,128)}) %reduce-scatter.53.cloned.1.call-update) | async-done | bytes 294928 | tf_op jit(solution)/shard_map/reduce_scatter | solution.py:325
  1173.6 62.9 %reduce-scatter.51.cloned.1.call-done = f32[96,192]{1,0:T(8,128)} async-done(((f32[768,192]{1,0:T(8,128)}), f32[96,192]{1,0:T(8,128)}) %reduce-scatter.51.cloned.1.call-update) | async-done | bytes 73744 | tf_op jit(solution)/shard_map/reduce_scatter | solution.py:355
  1236.5 65.0 %reduce-scatter.49.cloned.1.call-done = f32[96,192]{1,0:T(8,128)} async-done(((f32[768,192]{1,0:T(8,128)}), f32[96,192]{1,0:T(8,128)}) %reduce-scatter.49.cloned.1.call-update) | async-done | bytes 73744 | tf_op jit(solution)/shard_map/reduce_scatter | solution.py:355
  1303.1 63.6 %reduce-scatter.47.cloned.1.call-done = f32[96,192]{1,0:T(8,128)} async-done(((f32[768,192]{1,0:T(8,128)}), f32[96,192]{1,0:T(8,128)}) %reduce-scatter.47.cloned.1.call-update) | async-done | bytes 73744 | tf_op jit(solution)/shard_map/reduce_scatter | solution.py:352
  1366.7 64.8 %reduce-scatter.45.cloned.1.call-done = f32[96,192]{1,0:T(8,128)} async-done(((f32[768,192]{1,0:T(8,128)}), f32[96,192]{1,0:T(8,128)}) %reduce-scatter.45.cloned.1.call-update) | async-done | bytes 73744 | tf_op jit(solution)/shard_map/reduce_scatter | solution.py:352
  1433.1 63.7 %reduce-scatter.43.cloned.1.call-done = f32[96,192]{1,0:T(8,128)} async-done(((f32[768,192]{1,0:T(8,128)}), f32[96,192]{1,0:T(8,128)}) %reduce-scatter.43.cloned.1.call-update) | async-done | bytes 73744 | tf_op jit(solution)/shard_map/reduce_scatter | solution.py:349
  1496.8 64.8 %reduce-scatter.41.cloned.1.call-done = f32[96,192]{1,0:T(8,128)} async-done(((f32[768,192]{1,0:T(8,128)}), f32[96,192]{1,0:T(8,128)}) %reduce-scatter.41.cloned.1.call-update) | async-done | bytes 73744 | tf_op jit(solution)/shard_map/reduce_scatter | solution.py:349
  1563.2 63.4 %reduce-scatter.39.cloned.1.call-done = f32[96,192]{1,0:T(8,128)} async-done(((f32[768,192]{1,0:T(8,128)}), f32[96,192]{1,0:T(8,128)}) %reduce-scatter.39.cloned.1.call-update) | async-done | bytes 73744 | tf_op jit(solution)/shard_map/reduce_scatter | solution.py:346
  1626.6 64.8 %reduce-scatter.37.cloned.1.call-done = f32[96,192]{1,0:T(8,128)} async-done(((f32[768,192]{1,0:T(8,128)}), f32[96,192]{1,0:T(8,128)}) %reduce-scatter.37.cloned.1.call-update) | async-done | bytes 73744 | tf_op jit(solution)/shard_map/reduce_scatter | solution.py:346
  1693.0 30.8 %reduce-scatter.35.cloned.1.call-done = bf16[1024,192]{0,1:T(8,128)(2,1)} async-done(((bf16[1024,768]{0,1:T(8,128)(2,1)}), bf16[1024,192]{0,1:T(8,128)(2,1)}) %reduce-scatter.35.cloned.1.call-update) | async-done | bytes 393232 | tf_op jit(solution)/shard_map/reduce_scatter | solution.py:83
  1725.3 23.4 %all-reduce.32 = (f32[192]{0:T(256)S(1)}, f32[192]{0:T(256)S(1)}, f32[192]{0:T(256)S(1)}, f32[192]{0:T(256)S(1)}, f32[192]{0:T(256)S(1)}, /*index=5*/f32[192]{0:...) all-reduce(f32[192]{0:T(256)S(1)} %reduce_sum.413, ...), channel_id=41, replica_groups=mesh['row'=8,'col'=4] {'row'}, use_global_device_ids=true, to_apply=%region_63.64.clone | all-reduce | flops 4608 | bytes 36864
  1750.0 12.4 all-reduce.33
  (500 shorter events, 172.5 us)
Async XLA Ops:
  8.0 90.5 %copy-start.62 = (bf16[2,96,192]{2,1,0:T(8,128)(2,1)S(1)}, bf16[2,96,192]{2,1,0:T(8,128)(2,1)}, u32[]{:S(2)}) copy-start(bf16[2,96,192]{2,1,0:T(8,128)(2,1)} %param.20) | copy-start | bytes 221188
  8.0 115.8 %copy-start.63 = (bf16[2,96,192]{2,1,0:T(8,128)(2,1)S(1)}, bf16[2,96,192]{2,1,0:T(8,128)(2,1)}, u32[]{:S(2)}) copy-start(bf16[2,96,192]{2,1,0:T(8,128)(2,1)} %param.19) | copy-start | bytes 221188
  8.1 142.9 %all-gather.35.cloned.1.call-start = ((), (), s32[]{:S(2)}) async-start(), calls=%async_computation.20 | async-start | bytes 1966080 | tf_op jit(solution)/shard_map/all_gather | solution.py:55
  20.3 208.0 %reduce-scatter.21.cloned.1.call-start = ((), (), s32[]{:S(2)}) async-start(), calls=%async_computation.21 | async-start | bytes 1966080 | tf_op jit(solution)/shard_map/reduce_scatter | solution.py:68
  167.5 75.0 %all-gather.51.cloned.1.call-start = ((), (), s32[]{:S(2)}) async-start(), calls=%async_computation.48 | async-start | bytes 1327104 | tf_op jit(solution)/shard_map/all_gather | solution.py:254
  169.3 96.1 %all-gather.37.cloned.1.call-start = ((), (), s32[]{:S(2)}) async-start(), calls=%async_computation.22 | async-start | bytes 1966080 | tf_op jit(solution)/shard_map/all_gather | solution.py:55
  170.1 100.2 %copy-start.87 = (f32[1,192]{1,0:T(1,128)}, f32[1,192]{1,0:T(1,128)S(1)}, u32[]{:S(2)}) copy-start(f32[1,192]{1,0:T(1,128)S(1)} %fusion.170) | copy-start | bytes 2308
  239.2 67.6 %all-gather.53.cloned.1.call-start = ((), (), s32[]{:S(2)}) async-start(), calls=%async_computation.49 | async-start | bytes 1327104 | tf_op jit(solution)/shard_map/all_gather | solution.py:255
  241.0 100.3 %reduce-scatter.23.cloned.1.call-start = ((), (), s32[]{:S(2)}) async-start(), calls=%async_computation.23 | async-start | bytes 1966080 | tf_op jit(solution)/shard_map/reduce_scatter | solution.py:68
  311.8 150.0 %all-gather.39.cloned.1.call-start = ((), (), s32[]{:S(2)}) async-start(), calls=%async_computation.24 | async-start | bytes 1966080 | tf_op jit(solution)/shard_map/all_gather | solution.py:55
  312.0 151.9 %copy-start.93 = (f32[1,192]{1,0:T(1,128)}, f32[1,192]{1,0:T(1,128)S(1)}, u32[]{:S(2)}) copy-start(f32[1,192]{1,0:T(1,128)S(1)} %fusion.172) | copy-start | bytes 2308
  353.5 181.5 %reduce-scatter.25.cloned.1.call-start = ((), (), s32[]{:S(2)}) async-start(), calls=%async_computation.25 | async-start | bytes 1966080 | tf_op jit(solution)/shard_map/reduce_scatter | solution.py:68
  478.3 71.0 %all-gather.55.cloned.1.call-start = ((), (), s32[]{:S(2)}) async-start(), calls=%async_computation.50 | async-start | bytes 1327104 | tf_op jit(solution)/shard_map/all_gather | solution.py:254
  479.1 93.5 %all-gather.41.cloned.1.call-start = ((), (), s32[]{:S(2)}) async-start(), calls=%async_computation.26 | async-start | bytes 1966080 | tf_op jit(solution)/shard_map/all_gather | solution.py:55
  479.9 205.1 %copy-start.90 = (f32[1,192]{1,0:T(1,128)}, f32[1,192]{1,0:T(1,128)S(1)}, u32[]{:S(2)}) copy-start(f32[1,192]{1,0:T(1,128)S(1)} %fusion.174) | copy-start | bytes 2308
  544.3 140.6 %copy-start.57 = (f32[1024]{0:T(1024)}, f32[1024]{0:T(1024)S(1)}, u32[]{:S(2)}) copy-start(f32[1024]{0:T(1024)S(1)} %get-tuple-element.110) | copy-start | bytes 12292
  544.3 140.6 %copy-start.59 = (f32[1024]{0:T(1024)}, f32[1024]{0:T(1024)S(1)}, u32[]{:S(2)}) copy-start(f32[1024]{0:T(1024)S(1)} %get-tuple-element.111) | copy-start | bytes 12292
  546.5 67.5 %all-gather.57.cloned.1.call-start = ((), (), s32[]{:S(2)}) async-start(), calls=%async_computation.51 | async-start | bytes 1327104 | tf_op jit(solution)/shard_map/all_gather | solution.py:255
  547.0 89.5 %all-gather.43.cloned.1.call-start = ((), (), s32[]{:S(2)}) async-start(), calls=%async_computation.28 | async-start | bytes 1966080 | tf_op jit(solution)/shard_map/all_gather | solution.py:77
  547.6 127.9 %reduce-scatter.29.cloned.1.call-start = ((), (), s32[]{:S(2)}) async-start(), calls=%async_computation.29 | async-start | bytes 1966080 | tf_op jit(solution)/shard_map/reduce_scatter | solution.py:83
  548.6 88.0 %copy-start.105 = (f32[768]{0:T(1024)}, f32[768]{0:T(1024)S(1)}, u32[]{:S(2)}) copy-start(f32[768]{0:T(1024)S(1)} %convert_element_type.440) | copy-start | bytes 9220
  647.6 61.9 %all-gather.45.cloned.1.call-start = ((), (), s32[]{:S(2)}) async-start(), calls=%async_computation.30 | async-start | bytes 1966080 | tf_op jit(solution)/shard_map/all_gather | solution.py:77
  688.1 69.3 %reduce-scatter.31.cloned.1.call-start = ((), (), s32[]{:S(2)}) async-start(), calls=%async_computation.31 | async-start | bytes 1966080 | tf_op jit(solution)/shard_map/reduce_scatter | solution.py:83
  729.5 58.8 %reduce-scatter.27.cloned.1.call-start = ((), (), s32[]{:S(2)}) async-start(), calls=%async_computation.27 | async-start | bytes 1966080 | tf_op jit(solution)/shard_map/reduce_scatter | solution.py:68
  734.6 78.1 %all-gather.47.cloned.1.call-start = ((), (), s32[]{:S(2)}) async-start(), calls=%async_computation.32 | async-start | bytes 1966080 | tf_op jit(solution)/shard_map/all_gather | solution.py:77
  792.7 58.7 %reduce-scatter.33.cloned.1.call-start = ((), (), s32[]{:S(2)}) async-start(), calls=%async_computation.33 | async-start | bytes 1966080 | tf_op jit(solution)/shard_map/reduce_scatter | solution.py:83
  823.7 64.8 %all-gather.49.cloned.1.call-start = ((), (), s32[]{:S(2)}) async-start(), calls=%async_computation.34 | async-start | bytes 1966080 | tf_op jit(solution)/shard_map/all_gather | solution.py:77
  864.6 91.3 %reduce-scatter.59.cloned.1.call-start = ((), (), s32[]{:S(2)}) async-start(), calls=%async_computation.47 | async-start | bytes 2654208 | tf_op jit(solution)/shard_map/reduce_scatter | solution.py:326
  870.1 157.6 %reduce-scatter.57.cloned.1.call-start = ((), (), s32[]{:S(2)}) async-start(), calls=%async_computation.46 | async-start | bytes 2654208 | tf_op jit(solution)/shard_map/reduce_scatter | solution.py:326
  875.5 224.1 %reduce-scatter.55.cloned.1.call-start = ((), (), s32[]{:S(2)}) async-start(), calls=%async_computation.45 | async-start | bytes 2654208 | tf_op jit(solution)/shard_map/reduce_scatter | solution.py:325
  880.4 291.2 %reduce-scatter.53.cloned.1.call-start = ((), (), s32[]{:S(2)}) async-start(), calls=%async_computation.44 | async-start | bytes 2654208 | tf_op jit(solution)/shard_map/reduce_scatter | solution.py:325
  885.1 351.4 %reduce-scatter.51.cloned.1.call-start = ((), (), s32[]{:S(2)}) async-start(), calls=%async_computation.43 | async-start | bytes 884736 | tf_op jit(solution)/shard_map/reduce_scatter | solution.py:355
  888.4 413.1 %reduce-scatter.49.cloned.1.call-start = ((), (), s32[]{:S(2)}) async-start(), calls=%async_computation.42 | async-start | bytes 884736 | tf_op jit(solution)/shard_map/reduce_scatter | solution.py:355
  891.5 475.2 %reduce-scatter.47.cloned.1.call-start = ((), (), s32[]{:S(2)}) async-start(), calls=%async_computation.41 | async-start | bytes 884736 | tf_op jit(solution)/shard_map/reduce_scatter | solution.py:352
  896.0 535.5 %reduce-scatter.45.cloned.1.call-start = ((), (), s32[]{:S(2)}) async-start(), calls=%async_computation.40 | async-start | bytes 884736 | tf_op jit(solution)/shard_map/reduce_scatter | solution.py:352
  905.9 590.9 %reduce-scatter.43.cloned.1.call-start = ((), (), s32[]{:S(2)}) async-start(), calls=%async_computation.39 | async-start | bytes 884736 | tf_op jit(solution)/shard_map/reduce_scatter | solution.py:349
  908.9 652.6 %reduce-scatter.41.cloned.1.call-start = ((), (), s32[]{:S(2)}) async-start(), calls=%async_computation.38 | async-start | bytes 884736 | tf_op jit(solution)/shard_map/reduce_scatter | solution.py:349
  921.5 705.1 %reduce-scatter.39.cloned.1.call-start = ((), (), s32[]{:S(2)}) async-start(), calls=%async_computation.37 | async-start | bytes 884736 | tf_op jit(solution)/shard_map/reduce_scatter | solution.py:346
  924.5 766.9 %reduce-scatter.37.cloned.1.call-start = ((), (), s32[]{:S(2)}) async-start(), calls=%async_computation.36 | async-start | bytes 884736 | tf_op jit(solution)/shard_map/reduce_scatter | solution.py:346
  930.4 793.4 %reduce-scatter.35.cloned.1.call-start = ((), (), s32[]{:S(2)}) async-start(), calls=%async_computation.35 | async-start | bytes 1966080 | tf_op jit(solution)/shard_map/reduce_scatter | solution.py:83
  933.7 239.7 %copy-start.98 = (f32[3,64]{1,0:T(4,128)S(1)}, f32[3,64]{1,0:T(4,128)}, u32[]{:S(2)}) copy-start(f32[3,64]{1,0:T(4,128)} %get-tuple-element.156) | copy-start | bytes 2308
  933.7 790.1 %copy-start.67 = (f32[1024]{0:T(1024)S(1)}, f32[1024]{0:T(1024)}, u32[]{:S(2)}) copy-start(f32[1024]{0:T(1024)} %copy-done.66) | copy-start | bytes 12292
  933.7 790.1 %copy-start.69 = (f32[1024]{0:T(1024)S(1)}, f32[1024]{0:T(1024)}, u32[]{:S(2)}) copy-start(f32[1024]{0:T(1024)} %copy-done.68) | copy-start | bytes 12292
  933.7 790.1 %copy-start.92 = (f32[1,192]{1,0:T(1,128)S(1)}, f32[1,192]{1,0:T(1,128)}, u32[]{:S(2)}) copy-start(f32[1,192]{1,0:T(1,128)} %copy-done.91) | copy-start | bytes 2308
  933.7 791.5 %copy-start.99 = (f32[192]{0:T(256)S(1)}, f32[192]{0:T(256)}, u32[]{:S(2)}) copy-start(f32[192]{0:T(256)} %get-tuple-element.88) | copy-start | bytes 2308
  933.7 791.5 %copy-start.100 = (f32[192]{0:T(256)S(1)}, f32[192]{0:T(256)}, u32[]{:S(2)}) copy-start(f32[192]{0:T(256)} %get-tuple-element.97) | copy-start | bytes 2308
  933.7 791.5 %copy-start.101 = (f32[192]{0:T(256)S(1)}, f32[192]{0:T(256)}, u32[]{:S(2)}) copy-start(f32[192]{0:T(256)} %get-tuple-element.83) | copy-start | bytes 2308
  933.8 791.5 %copy-start.102 = (f32[192]{0:T(256)S(1)}, f32[192]{0:T(256)}, u32[]{:S(2)}) copy-start(f32[192]{0:T(256)} %get-tuple-element.86) | copy-start | bytes 2308
  933.8 791.5 %copy-start.106 = (f32[768]{0:T(1024)S(1)}, f32[768]{0:T(1024)}, u32[]{:S(2)}) copy-start(f32[768]{0:T(1024)} %get-tuple-element.158) | copy-start | bytes 9220
  933.8 791.5 %copy-start.107 = (f32[768]{0:T(1024)S(1)}, f32[768]{0:T(1024)}, u32[]{:S(2)}) copy-start(f32[768]{0:T(1024)} %get-tuple-element.160) | copy-start | bytes 9220
  933.8 791.5 %copy-start.108 = (f32[192]{0:T(256)S(1)}, f32[192]{0:T(256)}, u32[]{:S(2)}) copy-start(f32[192]{0:T(256)} %get-tuple-element.19) | copy-start | bytes 2308
  933.8 791.4 %copy-start.109 = (f32[192]{0:T(256)S(1)}, f32[192]{0:T(256)}, u32[]{:S(2)}) copy-start(f32[192]{0:T(256)} %get-tuple-element.36) | copy-start | bytes 2308
  933.8 791.4 %copy-start.110 = (f32[192]{0:T(256)S(1)}, f32[192]{0:T(256)}, u32[]{:S(2)}) copy-start(f32[192]{0:T(256)} %get-tuple-element.21) | copy-start | bytes 2308
  933.8 791.4 %copy-start.111 = (f32[192]{0:T(256)S(1)}, f32[192]{0:T(256)}, u32[]{:S(2)}) copy-start(f32[192]{0:T(256)} %get-tuple-element.38) | copy-start | bytes 2308
  933.8 791.4 %copy-start.112 = (f32[192]{0:T(256)S(1)}, f32[192]{0:T(256)}, u32[]{:S(2)}) copy-start(f32[192]{0:T(256)} %get-tuple-element.17) | copy-start | bytes 2308
  933.9 791.4 %copy-start.113 = (f32[192]{0:T(256)S(1)}, f32[192]{0:T(256)}, u32[]{:S(2)}) copy-start(f32[192]{0:T(256)} %get-tuple-element.35) | copy-start | bytes 2308
  933.9 833.8 %copy-start.11 = (bf16[1024,192]{0,1:T(8,128)(2,1)S(1)}, bf16[1024,192]{0,1:T(8,128)(2,1)}, u32[]{:S(2)}) copy-start(bf16[1024,192]{0,1:T(8,128)(2,1)} %reduce-scatter.21.cloned.1.call-done) | copy-start | bytes 1179652
  933.9 833.7 %copy-start.12 = (f32[1024,192]{0,1:T(8,128)S(1)}, f32[1024,192]{0,1:T(8,128)}, u32[]{:S(2)}) copy-start(f32[1024,192]{0,1:T(8,128)} %get-tuple-element.85) | copy-start | bytes 2359300
  933.9 833.7 %copy-start.18 = (bf16[1024,192]{0,1:T(8,128)(2,1)S(1)}, bf16[1024,192]{0,1:T(8,128)(2,1)}, u32[]{:S(2)}) copy-start(bf16[1024,192]{0,1:T(8,128)(2,1)} %reduce-scatter.33.cloned.1.call-done) | copy-start | bytes 1179652
  933.9 833.7 %copy-start.53 = (f32[1024]{0:T(1024)S(1)}, f32[1024]{0:T(1024)}, u32[]{:S(2)}) copy-start(f32[1024]{0:T(1024)} %copy-done.51) | copy-start | bytes 12292
  933.9 833.7 %copy-start.56 = (f32[1024]{0:T(1024)S(1)}, f32[1024]{0:T(1024)}, u32[]{:S(2)}) copy-start(f32[1024]{0:T(1024)} %copy-done.54) | copy-start | bytes 12292
  933.9 833.7 %copy-start.75 = (f32[1024]{0:T(1024)S(1)}, f32[1024]{0:T(1024)}, u32[]{:S(2)}) copy-start(f32[1024]{0:T(1024)} %copy-done.74) | copy-start | bytes 12292
  933.9 833.7 %copy-start.77 = (f32[1024]{0:T(1024)S(1)}, f32[1024]{0:T(1024)}, u32[]{:S(2)}) copy-start(f32[1024]{0:T(1024)} %copy-done.76) | copy-start | bytes 12292
  933.9 833.7 %copy-start.89 = (f32[1,192]{1,0:T(1,128)S(1)}, f32[1,192]{1,0:T(1,128)}, u32[]{:S(2)}) copy-start(f32[1,192]{1,0:T(1,128)} %copy-done.87) | copy-start | bytes 2308
  (91 other events, 791.9 us)
Sparse Core Ops, SparseCore 0:
  20.5 21.5 all-gather.34
  167.6 60.6 reduce-scatter.20
  312.0 29.3 reduce-scatter.22
  478.4 56.5 reduce-scatter.24
  647.7 27.7 reduce-scatter.28
  688.2 21.2 all-gather.44
  729.6 27.7 reduce-scatter.30
  760.1 28.1 reduce-scatter.26
Sparse Core Ops, SparseCore 1:
  171.0 71.2 all-gather.50
  244.4 21.0 all-gather.36
  268.3 38.4 all-gather.52
  353.5 21.0 all-gather.38
  482.1 67.1 all-gather.54
  551.5 21.0 all-gather.40
  575.5 38.4 all-gather.56
  615.5 21.0 all-gather.42
  792.8 19.9 all-gather.46
  823.8 27.6 reduce-scatter.32
  864.7 21.0 all-gather.48
  889.6 66.3 reduce-scatter.58
  959.7 67.9 reduce-scatter.56
  1031.6 67.9 reduce-scatter.54
  1103.5 67.9 reduce-scatter.52
  1175.2 61.3 reduce-scatter.50
  1239.8 61.6 reduce-scatter.48
  1305.2 61.5 reduce-scatter.46
  1369.9 61.6 reduce-scatter.44
  1435.2 61.6 reduce-scatter.42
  1500.0 61.5 reduce-scatter.40
  1565.1 61.5 reduce-scatter.38
  1629.8 61.6 reduce-scatter.36
  1694.1 29.6 reduce-scatter.34
where the time goes:
time: 1790 us; the launch traced here: 1780 us
  waiting for transfers between devices  1200 us (67%)
  blocking collectives  303 us (17%)
  matrix products  138 us (8%)
  other arithmetic  81.3 us (5%)
  local copies, waits for them, and re-layouts  32.7 us (2%)
  between operations  20.6 us (1%)
    reduce_scatter x4, waiting for transfers between devices, branch_join(): lax.psum_scatter(partial_rows.astype(jnp.bfloat16), 'col', scatter_dimens...  160 us
    reduce_scatter x2, waiting for transfers between devices, local(): lax.psum_scatter(expand_part, 'row', scatter_dimension=0, tiled=True)  142 us
    reduce_scatter x2, waiting for transfers between devices, local(): lax.psum_scatter(contract_rows(norm_one, d_key), 'row', scatter_dimension...  128 us
    reduce_scatter x2, waiting for transfers between devices, local(): lax.psum_scatter(contract_rows(norm_one, d_value), 'row', scatter_dimensi...  128 us
    reduce_scatter x2, waiting for transfers between devices, local(): lax.psum_scatter(contract_rows(norm_one, d_query), 'row', scatter_dimensi...  128 us
    reduce_scatter x2, waiting for transfers between devices, local(): lax.psum_scatter(out_part, 'row', scatter_dimension=0, tiled=True)  128 us
    reduce_scatter x4, waiting for transfers between devices, norm_back(): lax.psum_scatter(feature_part.astype(jnp.bfloat16), 'col', scatter_dimens...  109 us
    reduce_scatter x2, waiting for transfers between devices, local(): lax.psum_scatter(contract_part, 'row', scatter_dimension=0, tiled=True)  92.1 us
  transfers between devices with their start and end apart: 32, of which 28 were waited for; matrix products, arithmetic and copies ran while one was open for 7% of the time, Pallas kernels for 0%

commit v1 on v0

v1 whole, which is shorter than its diff:
```python
import jax
import jax.numpy as jnp
from jax import lax
from jax.sharding import PartitionSpec as P

HD = 64
SEQ = 1024


EPSILON = 1e-05
NEG_FILL = -1e30


def contract_rows(left, right):
    return lax.dot_general(
        left, right, (((0,), (0,)), ((), ())), preferred_element_type=jnp.float32
    )


def contract_cols(left, right):
    return lax.dot_general(
        left, right, (((1,), (1,)), ((), ())), preferred_element_type=jnp.float32
    )


def gelu_tanh(values):
    return (
        0.5
        * values
        * (1.0 + jnp.tanh(0.7978845608028654 * (values + 0.044715 * values * values * values)))
    )


def col_gather(rows_in):
    return lax.all_gather(rows_in, "col", axis=0, tiled=True)


def col_scatter(partial_rows):
    return lax.psum_scatter(
        partial_rows.astype(jnp.bfloat16), "col", scatter_dimension=0, tiled=True
    ).astype(jnp.float32)


def own_rows(rows_in):
    count = rows_in.shape[0] // lax.axis_size("col")
    return lax.dynamic_slice_in_dim(rows_in, lax.axis_index("col") * count, count, 0)


def own_features(rows_in):
    width = rows_in.shape[-1] // lax.axis_size("col")
    return lax.dynamic_slice_in_dim(
        rows_in, lax.axis_index("col") * width, width, rows_in.ndim - 1
    )


def spread_bias(bias_share, full_width):
    return lax.dynamic_update_slice_in_dim(
        jnp.zeros((full_width,), jnp.float32),
        bias_share.astype(jnp.float32),
        lax.axis_index("col") * bias_share.shape[0],
        0,
    )


def norm_unit(rows_in):
    row_mean = jnp.mean(rows_in, axis=1, keepdims=True)
    centred = rows_in - row_mean
    inv_std = lax.rsqrt(jnp.mean(centred * centred, axis=1, keepdims=True) + EPSILON)
    return centred * inv_std, inv_std


def norm_apply(unit_rows, gain, shift):
    return (unit_rows * gain + shift).astype(jnp.bfloat16)


def norm_back(normed_grad, unit_rows, inv_std, gain):
    scaled = normed_grad * gain
    first = jnp.mean(scaled, axis=1, keepdims=True)
    second = jnp.mean(scaled * unit_rows, axis=1, keepdims=True)
    back_rows = inv_std * (scaled - first - unit_rows * second)
    return back_rows, jnp.sum(normed_grad * unit_rows, axis=0), jnp.sum(normed_grad, axis=0)


def token_sum(rows_in):
    return jnp.sum(rows_in.astype(jnp.float32), axis=0)


def by_row(vector):
    return vector.reshape(lax.axis_size("row"), -1)


def row_total(packed):
    return lax.psum_scatter(
        packed.astype(jnp.bfloat16), "row", scatter_dimension=0, tiled=True
    ).astype(jnp.float32)


def local(
    inputs,
    cotangent,
    query_weight,
    key_weight,
    value_weight,
    out_weight,
    query_bias,
    value_bias,
    out_bias,
    attention_gain,
    attention_shift,
    expand_weight,
    expand_bias,
    contract_weight,
    contract_bias,
    feed_gain,
    feed_shift,
):
    layer_count, slab, part = query_weight.shape
    hidden_part = expand_weight.shape[2]
    row_count = lax.axis_size("row")
    width = slab * row_count
    bias_pack = jnp.concatenate(
        [
            item.reshape(layer_count, -1)
            for item in (query_bias, value_bias, out_bias, contract_bias, expand_bias)
        ],
        axis=1,
    )
    bias_len = bias_pack.size
    attn_width = 4 * part
    bias_rows = -(-bias_len // (attn_width * 16)) * 16
    bias_block = jnp.pad(
        bias_pack.reshape(-1), (0, bias_rows * attn_width - bias_len)
    ).reshape(bias_rows, attn_width)

    def attn_slab(layer_idx):
        return jnp.concatenate(
            [
                query_weight[layer_idx],
                key_weight[layer_idx],
                value_weight[layer_idx],
                out_weight[layer_idx],
            ],
            axis=1,
        )

    first_pack = lax.all_gather(
        jnp.concatenate([attn_slab(0), bias_block], axis=0), "row", axis=0
    )
    gathered_bias = (
        first_pack[:, slab:].reshape(row_count, -1)[:, :bias_len].reshape(row_count, layer_count, -1)
    )
    small = part // row_count
    rest = [("feed", 0)]
    for layer_idx in range(1, layer_count):
        rest += [("attn", layer_idx), ("feed", layer_idx)]
    feed_slabs = [
        jnp.concatenate([expand_weight[item], contract_weight[item]], axis=1)
        for item in range(layer_count)
    ]
    attn_w = [first_pack[:, :slab].reshape(width, attn_width)]
    feed_w = [lax.all_gather(feed_slabs[0], "row", axis=0, tiled=True)]
    for layer_idx in range(1, layer_count):
        both = lax.all_gather(
            jnp.concatenate([attn_slab(layer_idx), feed_slabs[layer_idx]], axis=1),
            "row",
            axis=0,
            tiled=True,
        )
        attn_w.append(both[:, :attn_width])
        feed_w.append(both[:, attn_width:])

    def bias_of(layer_idx, start, count):
        return gathered_bias[:, layer_idx, start : start + count].reshape(-1)

    x_full = lax.all_gather(inputs, "col", axis=0, tiled=True).T
    cot_full = lax.all_gather(cotangent, "col", axis=0, tiled=True).T
    resid = own_rows(x_full).astype(jnp.float32)
    saved = []
    for layer_idx in range(layer_count):
        w_attn, w_feed = attn_w[layer_idx], feed_w[layer_idx]
        w_qkv, w_out = w_attn[:, : 3 * part], w_attn[:, 3 * part :]
        w_expand, w_contract = w_feed[:, :hidden_part], w_feed[:, hidden_part:]
        b_query = bias_of(layer_idx, 0, small).astype(jnp.float32)
        b_value = bias_of(layer_idx, small, small).astype(jnp.float32)
        b_out = bias_of(layer_idx, 2 * small, small)
        b_contract = bias_of(layer_idx, 3 * small, small)
        b_expand = bias_of(layer_idx, 4 * small, hidden_part // row_count)
        gain_one = attention_gain[layer_idx].astype(jnp.float32)
        shift_one = attention_shift[layer_idx].astype(jnp.float32)
        gain_two = feed_gain[layer_idx].astype(jnp.float32)
        shift_two = feed_shift[layer_idx].astype(jnp.float32)
        unit_one, inv_one = norm_unit(resid)
        if layer_idx == 0:
            norm_one = norm_apply(norm_unit(x_full.astype(jnp.float32))[0], gain_one, shift_one)
        else:
            norm_one = col_gather(norm_apply(unit_one, gain_one, shift_one))
        b_qkv = jnp.concatenate([b_query, jnp.zeros_like(b_query), b_value])
        qkv = (jnp.dot(norm_one, w_qkv, preferred_element_type=jnp.float32) + b_qkv).astype(
            jnp.bfloat16
        )
        query_rows, key_rows, value_rows = (
            qkv[:, :part],
            qkv[:, part : 2 * part],
            qkv[:, 2 * part :],
        )
        mixed_rows, log_totals = attend(query_rows, key_rows, value_rows)
        resid = resid + col_scatter(contract_cols(mixed_rows, w_out) + spread_bias(b_out, width))
        unit_two, inv_two = norm_unit(resid)
        norm_two = col_gather(norm_apply(unit_two, gain_two, shift_two))
        before_act = jnp.dot(norm_two, w_expand, preferred_element_type=jnp.float32) + b_expand
        hidden_rows = gelu_tanh(before_act).astype(jnp.bfloat16)
        partial_rows = contract_cols(hidden_rows, w_contract) + spread_bias(b_contract, width)
        if layer_idx + 1 < layer_count:
            resid = resid + col_scatter(partial_rows)
        else:
            count = resid.shape[0]
            start = lax.axis_index("col") * count
            mine = lax.dynamic_slice_in_dim(partial_rows, start, count, 0) + resid
            partial_rows = lax.dynamic_update_slice_in_dim(partial_rows, mine, start, 0)
            outputs = lax.psum_scatter(
                partial_rows.astype(jnp.bfloat16), "col", scatter_dimension=1, tiled=True
            ).T
        saved.append(
            (
                (w_qkv, w_out, w_expand, w_contract, gain_one, gain_two),
                (norm_one, unit_one, inv_one, query_rows, key_rows, value_rows),
                (mixed_rows, log_totals, norm_two, unit_two, inv_two, before_act, hidden_rows),
            )
        )
    grad = own_rows(cot_full).astype(jnp.float32)
    branch_full = cot_full
    packs = [None] * layer_count
    vectors = [None] * layer_count
    norm_sums = [None] * layer_count
    for layer_idx in reversed(range(layer_count)):
        (
            (w_qkv, w_out, w_expand, w_contract, gain_one, gain_two),
            (norm_one, unit_one, inv_one, query_rows, key_rows, value_rows),
            (mixed_rows, log_totals, norm_two, unit_two, inv_two, before_act, hidden_rows),
        ) = saved[layer_idx]
        d_hidden = jnp.dot(branch_full, w_contract, preferred_element_type=jnp.float32)
        d_before = jax.vjp(gelu_tanh, before_act)[1](d_hidden)[0].astype(jnp.bfloat16)
        d_norm = col_scatter(contract_cols(d_before, w_expand))
        contract_part = contract_rows(branch_full, hidden_rows)
        expand_part = contract_rows(norm_two, d_before)
        contract_bias_part = token_sum(own_features(branch_full))
        back_rows, gain_two_part, shift_two_part = norm_back(d_norm, unit_two, inv_two, gain_two)
        grad = grad + back_rows
        branch_full = col_gather(grad.astype(jnp.bfloat16))
        d_mixed = jnp.dot(branch_full, w_out, preferred_element_type=jnp.float32).astype(
            jnp.bfloat16
        )
        out_part = contract_rows(branch_full, mixed_rows)
        out_bias_part = token_sum(own_features(branch_full))
        d_query, d_key, d_value = attend_back(query_rows, key_rows, value_rows, log_totals, d_mixed)
        d_qkv = jnp.concatenate([d_query, d_key, d_value], axis=1)
        d_norm = col_scatter(contract_cols(d_qkv, w_qkv))
        qkv_part = contract_rows(norm_one, d_qkv)
        back_rows, gain_one_part, shift_one_part = norm_back(d_norm, unit_one, inv_one, gain_one)
        grad = grad + back_rows
        branch_full = col_gather(grad.astype(jnp.bfloat16))
        packs[layer_idx] = jnp.concatenate([qkv_part, out_part, expand_part, contract_part], axis=1)
        vectors[layer_idx] = (
            token_sum(d_query),
            token_sum(d_value),
            out_bias_part,
            token_sum(d_before),
            contract_bias_part,
        )
        norm_sums[layer_idx] = jnp.stack(
            [gain_one_part, shift_one_part, gain_two_part, shift_two_part]
        )
    inputs_grad = own_features(branch_full).astype(jnp.float32).T
    norm_total = own_features(lax.psum(jnp.stack(norm_sums), "col"))
    flat = []
    for layer_idx in range(layer_count):
        flat += [by_row(item) for item in vectors[layer_idx]]
        flat += [by_row(norm_total[layer_idx, item]) for item in range(4)]
    sizes = [item.shape[1] for item in flat]
    flat = jnp.concatenate(flat, axis=1)
    pack_width = packs[0].shape[1]
    extra = -(-flat.shape[1] // (pack_width * 16)) * 16
    flat = jnp.pad(flat, ((0, 0), (0, extra * pack_width - flat.shape[1])))
    last_pack = jnp.concatenate(
        [
            packs[0].reshape(row_count, slab, pack_width),
            flat.reshape(row_count, extra, pack_width),
        ],
        axis=1,
    )
    last_total = row_total(last_pack)[0]
    totals = [last_total[:slab]] + [row_total(packs[item]) for item in range(1, layer_count)]
    loose = last_total[slab:].reshape(-1)
    pieces = []
    start = 0
    for size in sizes:
        pieces.append(loose[start : start + size])
        start += size

    def weight_grad(start, count):
        return jnp.stack([item[:, start : start + count] for item in totals])

    def vector_grad(member):
        return jnp.stack([pieces[layer * 9 + member].reshape(1, -1) for layer in range(layer_count)])

    return (
        outputs,
        inputs_grad,
        weight_grad(0, part),
        weight_grad(part, part),
        weight_grad(2 * part, part),
        weight_grad(3 * part, part),
        vector_grad(0),
        vector_grad(1),
        vector_grad(2),
        vector_grad(5),
        vector_grad(6),
        weight_grad(4 * part, hidden_part),
        vector_grad(3),
        weight_grad(4 * part + hidden_part, hidden_part),
        vector_grad(4),
        vector_grad(7),
        vector_grad(8),
    )


def split_heads(rows_in):
    return rows_in.reshape(rows_in.shape[0] // SEQ, SEQ, rows_in.shape[1] // HD, HD)


def causal_scores(query_block, key_block, row_begin):
    scores = (
        jnp.einsum("sqhd,skhd->shqk", query_block, key_block, preferred_element_type=jnp.float32)
        * 0.125
    )
    grid_shape = (query_block.shape[1], key_block.shape[1])
    row_ids = row_begin + lax.broadcasted_iota(jnp.int32, grid_shape, 0)
    col_ids = lax.broadcasted_iota(jnp.int32, grid_shape, 1)
    return jnp.where((row_ids >= col_ids)[None, None], scores, NEG_FILL)


def attend(query_rows, key_rows, value_rows):
    block_rows = min(512, SEQ)
    query_seq = split_heads(query_rows)
    key_seq = split_heads(key_rows)
    value_seq = split_heads(value_rows)
    out_blocks = []
    log_totals = []
    for row_begin in range(0, SEQ, block_rows):
        row_end = row_begin + block_rows
        scores = causal_scores(query_seq[:, row_begin:row_end], key_seq[:, :row_end], row_begin)
        row_top = jnp.max(scores, axis=-1, keepdims=True)
        weights = jnp.exp(scores - row_top)
        row_total = jnp.sum(weights, axis=-1, keepdims=True)
        prob_rows = (weights / row_total).astype(jnp.bfloat16)
        out_blocks.append(
            jnp.einsum(
                "shqk,skhd->sqhd",
                prob_rows,
                value_seq[:, :row_end],
                preferred_element_type=jnp.float32,
            )
        )
        log_totals.append(row_top + jnp.log(row_total))
    mixed_rows = jnp.concatenate(out_blocks, axis=1).reshape(query_rows.shape).astype(jnp.bfloat16)
    return (mixed_rows, log_totals)


def attend_back(query_rows, key_rows, value_rows, log_totals, d_mixed):
    block_rows = min(512, SEQ)
    query_seq = split_heads(query_rows)
    key_seq = split_heads(key_rows)
    value_seq = split_heads(value_rows)
    grad_seq = split_heads(d_mixed)
    d_query_blocks = []
    d_key_seq = jnp.zeros(key_seq.shape, jnp.float32)
    d_value_seq = jnp.zeros(value_seq.shape, jnp.float32)
    for block_idx, row_begin in enumerate(range(0, SEQ, block_rows)):
        row_end = row_begin + block_rows
        tail_pad = ((0, 0), (0, SEQ - row_end), (0, 0), (0, 0))
        scores = causal_scores(query_seq[:, row_begin:row_end], key_seq[:, :row_end], row_begin)
        prob_rows = jnp.exp(scores - log_totals[block_idx])
        grad_block = grad_seq[:, row_begin:row_end]
        d_probs = jnp.einsum(
            "sqhd,skhd->shqk",
            grad_block,
            value_seq[:, :row_end],
            preferred_element_type=jnp.float32,
        )
        d_value_seq = d_value_seq + jnp.pad(
            jnp.einsum(
                "shqk,sqhd->skhd",
                prob_rows.astype(jnp.bfloat16),
                grad_block,
                preferred_element_type=jnp.float32,
            ),
            tail_pad,
        )
        inner_sum = jnp.sum(d_probs * prob_rows, axis=-1, keepdims=True)
        d_scores = (prob_rows * (d_probs - inner_sum)).astype(jnp.bfloat16)
        d_query_blocks.append(
            jnp.einsum(
                "shqk,skhd->sqhd",
                d_scores,
                key_seq[:, :row_end],
                preferred_element_type=jnp.float32,
            )
            * 0.125
        )
        d_key_seq = d_key_seq + jnp.pad(
            jnp.einsum(
                "shqk,sqhd->skhd",
                d_scores,
                query_seq[:, row_begin:row_end],
                preferred_element_type=jnp.float32,
            )
            * 0.125,
            tail_pad,
        )
    rows_shape = query_rows.shape
    d_query = jnp.concatenate(d_query_blocks, axis=1).reshape(rows_shape).astype(jnp.bfloat16)
    return (
        d_query,
        d_key_seq.reshape(rows_shape).astype(jnp.bfloat16),
        d_value_seq.reshape(rows_shape).astype(jnp.bfloat16),
    )


def solution(mesh):
    placed = (
        P("col", "row"),
        P("col", "row"),
        P(None, "row", "col"),
        P(None, "row", "col"),
        P(None, "row", "col"),
        P(None, "row", "col"),
        P(None, "col", "row"),
        P(None, "col", "row"),
        P(None, "col", "row"),
        P(),
        P(),
        P(None, "row", "col"),
        P(None, "col", "row"),
        P(None, "row", "col"),
        P(None, "col", "row"),
        P(),
        P(),
    )
    return jax.shard_map(
        local,
        mesh=mesh,
        in_specs=placed,
        out_specs=(
            P("col", "row"),
            P("col", "row"),
            P(None, "row", "col"),
            P(None, "row", "col"),
            P(None, "row", "col"),
            P(None, "row", "col"),
            P(None, "col", "row"),
            P(None, "col", "row"),
            P(None, "col", "row"),
            P(None, "col", "row"),
            P(None, "col", "row"),
            P(None, "row", "col"),
            P(None, "col", "row"),
            P(None, "row", "col"),
            P(None, "col", "row"),
            P(None, "col", "row"),
            P(None, "col", "row"),
        ),
        check_vma=False,
    )
```

time: 1790 us -> 905 us (0.51)
  waiting for transfers between devices: 1200 us -> 608 us
  blocking collectives: 303 us -> 11 us
  local copies, waits for them, and re-layouts: 32.7 us -> 67.1 us
  matrix products: 138 us -> 106 us
    reduce_scatter x20 -> x9, waiting for transfers between devices: 1020 us -> 270 us  [the longest x7 146 us: col_scatter(): lax.psum_scatter(partial_rows.astype(jnp.bfloat16), 'col', scatter_dimens...]
    all_gather x8 -> x0, blocking collectives: 210 us -> none  [the longest x2 53.9 us: local(): lax.all_gather(value_weight[layer_idx], 'row', axis=0, tiled=True)]
    all_gather x12, waiting for transfers between devices: 182 us -> 318 us  [the longest x7 142 us: col_gather(): return lax.all_gather(rows_in, 'col', axis=0, tiled=True)]
    psum x8 -> x1, blocking collectives: 57 us -> 11 us  [local(): norm_total = own_features(lax.psum(jnp.stack(norm_sums), 'col'))]
    unnamed x2 -> x0, blocking collectives: 36.1 us -> none
    dot_general x12 -> x8, matrix products: 39.6 us -> 19.9 us  [contract_rows(): lax.dot_general(left, right, (((0,), (0,)), ((), ())), preferred_element_...]
    transpose x0 -> x1, waiting for transfers between devices: none -> 19 us  [local(): outputs = lax.psum_scatter(partial_rows.astype(jnp.bfloat16), 'col', scat...]
  transfers between devices with their start and end apart: 32 -> 22, of which waited for: 28 -> 21; matrix products, arithmetic and copies ran while one was open for 7% -> 15% of each run, Pallas kernels for 0% -> 0%
where the time goes in v1:
time: 905 us; the launch traced here: 893 us
  waiting for transfers between devices  608 us (67%)
  matrix products  106 us (12%)
  other arithmetic  82.2 us (9%)
  local copies, waits for them, and re-layouts  67.1 us (7%)
  between operations  16.3 us (2%)
  blocking collectives  11 us (1%)
    reduce_scatter x7, waiting for transfers between devices, col_scatter(): lax.psum_scatter(partial_rows.astype(jnp.bfloat16), 'col', scatter_dimens...  146 us
    all_gather x7, waiting for transfers between devices, col_gather(): return lax.all_gather(rows_in, 'col', axis=0, tiled=True)  142 us
    reduce_scatter x2, waiting for transfers between devices, row_total(): lax.psum_scatter(packed.astype(jnp.bfloat16), 'row', scatter_dimension=0,...  124 us
    all_gather x1, waiting for transfers between devices, local(): lax.all_gather(jnp.concatenate([attn_slab(layer_idx), feed_slabs[layer_id...  61.3 us
    all_gather x1, waiting for transfers between devices, local(): feed_w = [lax.all_gather(feed_slabs[0], 'row', axis=0, tiled=True)]  44.7 us
    all_gather x1, waiting for transfers between devices, local(): lax.all_gather(jnp.concatenate([attn_slab(0), bias_block], axis=0), 'row'...  39.4 us
    dot_general x8, matrix products, contract_cols(): lax.dot_general(left, right, (((1,), (1,)), ((), ())), preferred_element_...  28.4 us
    unnamed x212, local copies, waits for them, and re-layouts  25.6 us
  transfers between devices with their start and end apart: 22, of which 21 were waited for; matrix products, arithmetic and copies ran while one was open for 15% of the time, Pallas kernels for 0%

profile of v1, /device:TPU:11, one launch (start us, length us, event | category | flops | bytes accessed | tf_op | source)
XLA Modules:
  0.0 893.3 jit_solution(5807840608385517120)
XLA Ops:
  17.0 13.9 %all-gather.14.cloned.1.call-done = bf16[768,1024]{1,0:T(8,128)(2,1)} async-done(((bf16[192,1024]{1,0:T(8,128)(2,1)}), bf16[768,1024]{1,0:T(8,128)(2,1)}) %all-gather.14.cloned.1.call-update) | async-done | bytes 1572880 | tf_op jit(solution)/shard_map/all_gather | solution.py:175
  32.6 1.9 fusion.6
  34.5 39.4 %all-gather.36.cloned.1.call-done = bf16[896,768]{1,0:T(8,128)(2,1)} async-done(((bf16[112,768]{1,0:T(8,128)(2,1)}), bf16[896,768]{1,0:T(8,128)(2,1)}) %all-gather.36.cloned.1.call-update) | async-done | bytes 1376272 | tf_op jit(solution)/shard_map/all_gather | solution.py:146
  89.8 2.9 add_convert_fusion.2
  92.9 1.9 slice_bitcast_fusion.44
  98.3 1.8 constant_dynamic-slice_fusion.1
  101.3 20.0 %reduce-scatter.15.cloned.1.call-done = bf16[256,768]{1,0:T(8,128)(2,1)} async-done(((bf16[1024,768]{1,0:T(8,128)(2,1)}), bf16[256,768]{1,0:T(8,128)(2,1)}) %reduce-scatter.15.cloned.1.call-update) | async-done | bytes 393232 | tf_op jit(solution)/shard_map/reduce_scatter | solution.py:39
  124.3 2.0 add_convert_fusion.7
  129.6 44.7 %all-gather.18.cloned.1.call-done = bf16[768,1536]{1,0:T(8,128)(2,1)} async-done(((bf16[96,1536]{1,0:T(8,128)(2,1)}), bf16[768,1536]{1,0:T(8,128)(2,1)}) %all-gather.18.cloned.1.call-update) | async-done | bytes 2359312 | tf_op jit(solution)/shard_map/all_gather | solution.py:161
  174.3 22.7 %all-gather.16.cloned.1.call-done = bf16[1024,768]{1,0:T(8,128)(2,1)} async-done(((bf16[256,768]{1,0:T(8,128)(2,1)}), bf16[1024,768]{1,0:T(8,128)(2,1)}) %all-gather.16.cloned.1.call-update) | async-done | bytes 1572880 | tf_op jit(solution)/shard_map/all_gather | solution.py:35
  196.9 3.3 fusion.113
  201.9 3.3 add_convert_fusion.1
  205.2 2.0 concatenate.75
  207.3 25.8 %reduce-scatter.17.cloned.1.call-done = bf16[256,768]{1,0:T(8,128)(2,1)} async-done(((bf16[1024,768]{1,0:T(8,128)(2,1)}), bf16[256,768]{1,0:T(8,128)(2,1)}) %reduce-scatter.17.cloned.1.call-update) | async-done | bytes 393232 | tf_op jit(solution)/shard_map/reduce_scatter | solution.py:39
  237.4 61.3 %all-gather.22.cloned.1.call-done = bf16[768,2304]{1,0:T(8,128)(2,1)} async-done(((bf16[96,2304]{1,0:T(8,128)(2,1)}), bf16[768,2304]{1,0:T(8,128)(2,1)}) %all-gather.22.cloned.1.call-update) | async-done | bytes 3538960 | tf_op jit(solution)/shard_map/all_gather | solution.py:163
  298.6 23.2 %all-gather.20.cloned.1.call-done = bf16[1024,768]{1,0:T(8,128)(2,1)} async-done(((bf16[256,768]{1,0:T(8,128)(2,1)}), bf16[1024,768]{1,0:T(8,128)(2,1)}) %all-gather.20.cloned.1.call-update) | async-done | bytes 1572880 | tf_op jit(solution)/shard_map/all_gather | solution.py:35
  321.8 2.9 add_convert_fusion.3
  332.8 3.0 add_convert_fusion
  336.2 27.7 %reduce-scatter.19.cloned.1.call-done = bf16[256,768]{1,0:T(8,128)(2,1)} async-done(((bf16[1024,768]{1,0:T(8,128)(2,1)}), bf16[256,768]{1,0:T(8,128)(2,1)}) %reduce-scatter.19.cloned.1.call-update) | async-done | bytes 393232 | tf_op jit(solution)/shard_map/reduce_scatter | solution.py:39
  368.6 18.7 %all-gather.24.cloned.1.call-done = bf16[1024,768]{1,0:T(8,128)(2,1)} async-done(((bf16[256,768]{1,0:T(8,128)(2,1)}), bf16[1024,768]{1,0:T(8,128)(2,1)}) %all-gather.24.cloned.1.call-update) | async-done | bytes 1572880 | tf_op jit(solution)/shard_map/all_gather | solution.py:35
  387.3 4.8 fusion.105
  392.1 16.5 %all-gather.26.cloned.1.call-done = bf16[768,1024]{1,0:T(8,128)(2,1)} async-done(((bf16[192,1024]{1,0:T(8,128)(2,1)}), bf16[768,1024]{1,0:T(8,128)(2,1)}) %all-gather.26.cloned.1.call-update) | async-done | bytes 1572880 | tf_op jit(solution)/shard_map/all_gather | solution.py:176
  408.6 7.2 fusion.192
  417.0 3.9 convolution_convert_fusion.3
  422.7 1.9 copy.107
  426.1 6.1 convolution_add_fusion
  432.2 16.6 %reduce-scatter.21.cloned.1.call-done = bf16[256,768]{1,0:T(8,128)(2,1)} async-done(((bf16[1024,768]{1,0:T(8,128)(2,1)}), bf16[256,768]{1,0:T(8,128)(2,1)}) %reduce-scatter.21.cloned.1.call-update) | async-done | bytes 393232 | tf_op jit(solution)/shard_map/reduce_scatter | solution.py:39
  448.8 2.3 fusion.142
  451.0 3.2 fusion.179
  456.2 18.4 %all-gather.28.cloned.1.call-done = bf16[1024,768]{1,0:T(8,128)(2,1)} async-done(((bf16[256,768]{1,0:T(8,128)(2,1)}), bf16[1024,768]{1,0:T(8,128)(2,1)}) %all-gather.28.cloned.1.call-update) | async-done | bytes 1572880 | tf_op jit(solution)/shard_map/all_gather | solution.py:35
  474.6 2.5 convolution_convert_fusion.11
  477.1 2.5 fusion.70
  483.4 1.9 multiply_reduce_fusion.1
  491.8 3.9 convolution_convert_fusion.1
  495.7 27.9 %reduce-scatter.23.cloned.1.call-done = bf16[256,768]{1,0:T(8,128)(2,1)} async-done(((bf16[1024,768]{1,0:T(8,128)(2,1)}), bf16[256,768]{1,0:T(8,128)(2,1)}) %reduce-scatter.23.cloned.1.call-update) | async-done | bytes 393232 | tf_op jit(solution)/shard_map/reduce_scatter | solution.py:39
  523.6 2.3 fusion.143
  525.9 2.8 fusion.177
  528.9 20.0 %all-gather.30.cloned.1.call-done = bf16[1024,768]{1,0:T(8,128)(2,1)} async-done(((bf16[256,768]{1,0:T(8,128)(2,1)}), bf16[1024,768]{1,0:T(8,128)(2,1)}) %all-gather.30.cloned.1.call-update) | async-done | bytes 1572880 | tf_op jit(solution)/shard_map/all_gather | solution.py:35
  548.9 6.9 fusion.190
  557.0 2.7 convolution_convert_fusion.2
  559.9 27.7 %reduce-scatter.25.cloned.1.call-done = bf16[256,768]{1,0:T(8,128)(2,1)} async-done(((bf16[1024,768]{1,0:T(8,128)(2,1)}), bf16[256,768]{1,0:T(8,128)(2,1)}) %reduce-scatter.25.cloned.1.call-update) | async-done | bytes 393232 | tf_op jit(solution)/shard_map/reduce_scatter | solution.py:39
  587.7 2.4 fusion.144
  590.0 2.7 fusion.175
  594.5 18.5 %all-gather.32.cloned.1.call-done = bf16[1024,768]{1,0:T(8,128)(2,1)} async-done(((bf16[256,768]{1,0:T(8,128)(2,1)}), bf16[1024,768]{1,0:T(8,128)(2,1)}) %all-gather.32.cloned.1.call-update) | async-done | bytes 1572880 | tf_op jit(solution)/shard_map/all_gather | solution.py:35
  613.0 2.3 convolution_convert_fusion.10
  619.7 1.9 multiply_reduce_fusion
  628.1 2.7 convolution_convert_fusion
  631.1 3.0 convolution_convert_fusion.5
  634.2 2.3 fusion.45
  638.2 2.1 pad_maximum_fusion.2
  640.3 5.8 copy.103
  656.6 5.4 convolution_convert_fusion.6
  662.1 2.0 fusion.145
  664.1 2.1 fusion.127
  666.6 4.6 convolution_convert_fusion.7
  676.3 2.6 convolution_convert_fusion.9
  679.4 4.1 copy.88
  685.7 11.0 %psum.7 = bf16[2,4,768]{2,1,0:T(4,128)(2,1)S(1)} all-reduce(f32[2,4,768]{2,1,0:T(4,128)S(1)} %pad_maximum_fusion.19), channel_id=1, replica_groups=mesh['row'=8,'col'=4] {'col'}, use_global_device_ids=true, to_apply=%region_51.52 | all-reduce | flops 6144 | bytes 36864 | tf_op jit(solution)/shard_map/psum | solution.py:274
  698.5 4.3 pad_maximum_fusion
  702.8 2.0 convert_element_type.425
  706.6 35.4 %reduce-scatter.33.cloned.1.call-done = bf16[96,2304]{1,0:T(8,128)(2,1)} async-done(((bf16[768,2304]{1,0:T(8,128)(2,1)}), bf16[96,2304]{1,0:T(8,128)(2,1)}) %reduce-scatter.33.cloned.1.call-update) | async-done | bytes 442384 | tf_op jit(solution)/shard_map/reduce_scatter | solution.py:93
  743.1 20.5 %all-gather.34.cloned.1.call-done = bf16[1024,768]{1,0:T(8,128)(2,1)} async-done(((bf16[256,768]{1,0:T(8,128)(2,1)}), bf16[1024,768]{1,0:T(8,128)(2,1)}) %all-gather.34.cloned.1.call-update) | async-done | bytes 1572880 | tf_op jit(solution)/shard_map/all_gather | solution.py:35
  766.2 88.7 %reduce-scatter.29.cloned.1.call-done = bf16[1,112,2304]{2,1,0:T(8,128)(2,1)} async-done(((bf16[8,112,2304]{2,1,0:T(8,128)(2,1)}), bf16[1,112,2304]{2,1,0:T(8,128)(2,1)}) %reduce-scatter.29.cloned.1.call-update) | async-done | bytes 516112 | tf_op jit(solution)/shard_map/reduce_scatter | solution.py:93
  866.9 19.0 %reduce-scatter.31.cloned.1.call-done = bf16[192,1024]{1,0:T(8,128)(2,1)} async-done(((bf16[768,1024]{1,0:T(8,128)(2,1)}), bf16[192,1024]{1,0:T(8,128)(2,1)}) %reduce-scatter.31.cloned.1.call-update) | async-done | bytes 393232 | tf_op jit(solution)/shard_map/transpose | solution.py:222
  (434 shorter events, 127.7 us)
Async XLA Ops:
  7.2 23.6 %all-gather.14.cloned.1.call-start = ((), (), s32[]{:S(2)}) async-start(), calls=%async_computation.10 | async-start | bytes 1966080 | tf_op jit(solution)/shard_map/all_gather | solution.py:175
  7.9 66.0 %all-gather.36.cloned.1.call-start = ((), (), s32[]{:S(2)}) async-start(), calls=%async_computation.29 | async-start | bytes 1548288 | tf_op jit(solution)/shard_map/all_gather | solution.py:146
  12.8 108.5 %reduce-scatter.15.cloned.1.call-start = ((), (), s32[]{:S(2)}) async-start(), calls=%async_computation.11 | async-start | bytes 1966080 | tf_op jit(solution)/shard_map/reduce_scatter | solution.py:39
  13.6 64.7 %copy-start.52 = (f32[768]{0:T(1024)}, f32[768]{0:T(1024)S(1)}, u32[]{:S(2)}) copy-start(f32[768]{0:T(1024)S(1)} %get-tuple-element.108) | copy-start | bytes 9220
  13.6 221.1 %copy-start.47 = (f32[768]{0:T(1024)}, f32[768]{0:T(1024)S(1)}, u32[]{:S(2)}) copy-start(f32[768]{0:T(1024)S(1)} %get-tuple-element.107) | copy-start | bytes 9220
  15.0 63.3 %copy-start.82 = (f32[768]{0:T(1024)}, f32[768]{0:T(1024)S(1)}, u32[]{:S(2)}) copy-start(f32[768]{0:T(1024)S(1)} %get-tuple-element.110) | copy-start | bytes 9220
  30.8 47.5 %copy-start.8 = (bf16[768,1024]{1,0:T(8,128)(2,1)S(1)}, bf16[768,1024]{1,0:T(8,128)(2,1)}, u32[]{:S(2)}) copy-start(bf16[768,1024]{1,0:T(8,128)(2,1)} %all-gather.14.cloned.1.call-done) | copy-start | bytes 4718596
  32.6 47.0 %copy-start.79 = (f32[1024]{0:T(1024)}, f32[1024]{0:T(1024)S(1)}, u32[]{:S(2)}) copy-start(f32[1024]{0:T(1024)S(1)} %broadcast_multiply_fusion) | copy-start | bytes 12292
  34.5 45.1 %copy-start.85 = (f32[1024]{0:T(1024)}, f32[1024]{0:T(1024)S(1)}, u32[]{:S(2)}) copy-start(f32[1024]{0:T(1024)S(1)} %add_rsqrt_fusion) | copy-start | bytes 12292
  79.7 5.3 copy-start.17
  87.8 7.6 copy-start.27
  92.8 81.5 %all-gather.18.cloned.1.call-start = ((), (), s32[]{:S(2)}) async-start(), calls=%async_computation.13 | async-start | bytes 2654208 | tf_op jit(solution)/shard_map/all_gather | solution.py:161
  95.5 101.5 %all-gather.16.cloned.1.call-start = ((), (), s32[]{:S(2)}) async-start(), calls=%async_computation.12 | async-start | bytes 1966080 | tf_op jit(solution)/shard_map/all_gather | solution.py:35
  96.9 103.3 %copy-start.49 = (f32[768]{0:T(1024)}, f32[768]{0:T(1024)S(1)}, u32[]{:S(2)}) copy-start(f32[768]{0:T(1024)S(1)} %get-tuple-element.104) | copy-start | bytes 9220
  126.3 106.8 %reduce-scatter.17.cloned.1.call-start = ((), (), s32[]{:S(2)}) async-start(), calls=%async_computation.14 | async-start | bytes 1966080 | tf_op jit(solution)/shard_map/reduce_scatter | solution.py:39
  129.6 72.3 %copy-start.86 = (f32[768]{0:T(1024)S(1)}, f32[768]{0:T(1024)}, u32[]{:S(2)}) copy-start(f32[768]{0:T(1024)} %reshape.774) | copy-start | bytes 9220
  196.9 5.0 copy-start.90
  205.2 30.2 %copy-start.70 = (f32[768]{0:T(1024)S(1)}, f32[768]{0:T(1024)}, u32[]{:S(2)}) copy-start(f32[768]{0:T(1024)} %get-tuple-element.109) | copy-start | bytes 9220
  205.2 93.4 %all-gather.22.cloned.1.call-start = ((), (), s32[]{:S(2)}) async-start(), calls=%async_computation.16 | async-start | bytes 3981312 | tf_op jit(solution)/shard_map/all_gather | solution.py:163
  207.3 114.6 %all-gather.20.cloned.1.call-start = ((), (), s32[]{:S(2)}) async-start(), calls=%async_computation.15 | async-start | bytes 1966080 | tf_op jit(solution)/shard_map/all_gather | solution.py:35
  234.5 90.2 %copy-start.62 = (f32[256]{0:T(256)}, f32[256]{0:T(256)S(1)}, u32[]{:S(2)}) copy-start(f32[256]{0:T(256)S(1)} %broadcast_multiply_fusion.11) | copy-start | bytes 3076
  234.7 90.0 %copy-start.66 = (f32[256]{0:T(256)}, f32[256]{0:T(256)S(1)}, u32[]{:S(2)}) copy-start(f32[256]{0:T(256)S(1)} %add_rsqrt_fusion.3) | copy-start | bytes 3076
  236.3 127.5 %reduce-scatter.19.cloned.1.call-start = ((), (), s32[]{:S(2)}) async-start(), calls=%async_computation.17 | async-start | bytes 1966080 | tf_op jit(solution)/shard_map/reduce_scatter | solution.py:39
  237.4 87.3 %copy-start.83 = (f32[768]{0:T(1024)}, f32[768]{0:T(1024)S(1)}, u32[]{:S(2)}) copy-start(f32[768]{0:T(1024)S(1)} %dynamic_update_slice.25) | copy-start | bytes 9220
  324.9 5.4 copy-start.19
  332.8 33.3 %copy-start.51 = (f32[768]{0:T(1024)S(1)}, f32[768]{0:T(1024)}, u32[]{:S(2)}) copy-start(f32[768]{0:T(1024)} %get-tuple-element.103) | copy-start | bytes 9220
  332.8 33.3 %copy-start.71 = (f32[768]{0:T(1024)S(1)}, f32[768]{0:T(1024)}, u32[]{:S(2)}) copy-start(f32[768]{0:T(1024)} %get-tuple-element.105) | copy-start | bytes 9220
  335.9 51.4 %all-gather.24.cloned.1.call-start = ((), (), s32[]{:S(2)}) async-start(), calls=%async_computation.18 | async-start | bytes 1966080 | tf_op jit(solution)/shard_map/all_gather | solution.py:35
  367.1 41.5 %all-gather.26.cloned.1.call-start = ((), (), s32[]{:S(2)}) async-start(), calls=%async_computation.19 | async-start | bytes 1966080 | tf_op jit(solution)/shard_map/all_gather | solution.py:176
  367.8 80.9 %reduce-scatter.21.cloned.1.call-start = ((), (), s32[]{:S(2)}) async-start(), calls=%async_computation.20 | async-start | bytes 1966080 | tf_op jit(solution)/shard_map/reduce_scatter | solution.py:39
  368.6 40.0 %copy-start.88 = (f32[768]{0:T(1024)}, f32[768]{0:T(1024)S(1)}, u32[]{:S(2)}) copy-start(f32[768]{0:T(1024)S(1)} %reshape.783) | copy-start | bytes 9220
  420.8 53.8 %all-gather.28.cloned.1.call-start = ((), (), s32[]{:S(2)}) async-start(), calls=%async_computation.21 | async-start | bytes 1966080 | tf_op jit(solution)/shard_map/all_gather | solution.py:35
  454.3 69.3 %reduce-scatter.23.cloned.1.call-start = ((), (), s32[]{:S(2)}) async-start(), calls=%async_computation.22 | async-start | bytes 1966080 | tf_op jit(solution)/shard_map/reduce_scatter | solution.py:39
  474.6 5.0 copy-start.3
  474.6 5.0 copy-start.20
  491.8 31.8 %copy-start.48 = (f32[768]{0:T(1024)S(1)}, f32[768]{0:T(1024)}, u32[]{:S(2)}) copy-start(f32[768]{0:T(1024)} %copy-done.47) | copy-start | bytes 9220
  491.8 31.8 %copy-start.63 = (f32[256]{0:T(256)S(1)}, f32[256]{0:T(256)}, u32[]{:S(2)}) copy-start(f32[256]{0:T(256)} %copy-done.62) | copy-start | bytes 3076
  491.8 31.8 %copy-start.67 = (f32[256]{0:T(256)S(1)}, f32[256]{0:T(256)}, u32[]{:S(2)}) copy-start(f32[256]{0:T(256)} %copy-done.66) | copy-start | bytes 3076
  495.6 53.3 %copy-start.87 = (f32[768]{0:T(1024)S(1)}, f32[768]{0:T(1024)}, u32[]{:S(2)}) copy-start(f32[768]{0:T(1024)} %reshape.774) | copy-start | bytes 9220
  495.7 53.2 %all-gather.30.cloned.1.call-start = ((), (), s32[]{:S(2)}) async-start(), calls=%async_computation.23 | async-start | bytes 1966080 | tf_op jit(solution)/shard_map/all_gather | solution.py:35
  528.7 58.9 %reduce-scatter.25.cloned.1.call-start = ((), (), s32[]{:S(2)}) async-start(), calls=%async_computation.24 | async-start | bytes 1966080 | tf_op jit(solution)/shard_map/reduce_scatter | solution.py:39
  548.9 8.1 copy-start.91
  557.0 30.6 %copy-start.50 = (f32[768]{0:T(1024)S(1)}, f32[768]{0:T(1024)}, u32[]{:S(2)}) copy-start(f32[768]{0:T(1024)} %copy-done.49) | copy-start | bytes 9220
  557.0 30.6 %copy-start.61 = (f32[256]{0:T(256)S(1)}, f32[256]{0:T(256)}, u32[]{:S(2)}) copy-start(f32[256]{0:T(256)} %copy-done.60) | copy-start | bytes 3076
  557.0 30.6 %copy-start.65 = (f32[256]{0:T(256)S(1)}, f32[256]{0:T(256)}, u32[]{:S(2)}) copy-start(f32[256]{0:T(256)} %copy-done.64) | copy-start | bytes 3076
  559.7 53.2 %all-gather.32.cloned.1.call-start = ((), (), s32[]{:S(2)}) async-start(), calls=%async_computation.25 | async-start | bytes 1966080 | tf_op jit(solution)/shard_map/all_gather | solution.py:35
  559.9 32.8 %copy-start.68 = (f32[256]{0:T(256)}, f32[256]{0:T(256)S(1)}, u32[]{:S(2)}) copy-start(f32[256]{0:T(256)S(1)} %broadcast_multiply_fusion.3) | copy-start | bytes 3076
  592.8 69.3 %reduce-scatter.27.cloned.1.call-start = ((), (), s32[]{:S(2)}) async-start(), calls=%async_computation.26 | async-start | bytes 1966080 | tf_op jit(solution)/shard_map/reduce_scatter | solution.py:39
  630.8 111.1 %reduce-scatter.33.cloned.1.call-start = ((), (), s32[]{:S(2)}) async-start(), calls=%async_computation.31 | async-start | bytes 3981312 | tf_op jit(solution)/shard_map/reduce_scatter | solution.py:93
  646.1 7.1 copy-start.76
  646.1 7.1 copy-start.74
  646.2 117.5 %all-gather.34.cloned.1.call-start = ((), (), s32[]{:S(2)}) async-start(), calls=%async_computation.27 | async-start | bytes 1966080 | tf_op jit(solution)/shard_map/all_gather | solution.py:35
  656.6 5.4 copy-start.81
  656.6 5.4 copy-start.53
  656.6 5.4 copy-start.69
  656.6 7.5 copy-start.16
  666.2 6.1 copy-start.7
  666.2 9.6 %copy-start.28 = (bf16[1,1024,3,64]{1,3,2,0:T(8,128)(2,1)S(1)}, bf16[1,1024,3,64]{1,3,2,0:T(8,128)(2,1)}, u32[]{:S(2)}) copy-start(bf16[1,1024,3,64]{1,3,2,0:T(8,128)(2,1)} %copy-done.27) | copy-start | bytes 1179652
  666.2 10.1 %copy-start.9 = (bf16[768,1024]{1,0:T(8,128)(2,1)S(1)}, bf16[768,1024]{1,0:T(8,128)(2,1)}, u32[]{:S(2)}) copy-start(bf16[768,1024]{1,0:T(8,128)(2,1)} %all-gather.14.cloned.1.call-done) | copy-start | bytes 4718596
  666.3 188.7 %reduce-scatter.29.cloned.1.call-start = ((), (), s32[]{:S(2)}) async-start(), calls=%async_computation.28 | async-start | bytes 4644864 | tf_op jit(solution)/shard_map/reduce_scatter | solution.py:93
  666.6 4.6 copy-start.77
  666.6 5.2 copy-start.75
  679.4 5.5 copy-start.78
  702.7 183.2 %reduce-scatter.31.cloned.1.call-start = ((), (), s32[]{:S(2)}) async-start(), calls=%async_computation.30 | async-start | bytes 1966080 | tf_op jit(solution)/shard_map/transpose | solution.py:222
  (60 other events, 129.8 us)
Sparse Core Ops, SparseCore 0:
  9.6 21.1 all-gather.13
  33.6 40.2 all-gather.35
  92.9 28.3 reduce-scatter.14
  124.2 50.0 all-gather.17
  176.3 20.5 all-gather.15
  205.3 27.7 reduce-scatter.16
  235.9 62.7 all-gather.21
  300.8 20.9 all-gather.19
  336.0 27.7 reduce-scatter.18
  367.2 20.0 all-gather.23
  388.9 19.6 all-gather.25
  421.0 27.7 reduce-scatter.20
  454.4 20.1 all-gather.27
  495.8 27.7 reduce-scatter.22
  528.8 20.0 all-gather.29
  559.8 27.7 reduce-scatter.24
  592.9 20.0 all-gather.31
  630.9 27.7 reduce-scatter.26
  662.8 79.0 reduce-scatter.32
  744.0 19.6 all-gather.33
  767.7 87.2 reduce-scatter.28
  858.1 27.8 reduce-scatter.30

commit v2 on v1

--- a/solution.py
+++ b/solution.py
@@ -1,6 +1,10 @@
+import functools
+
 import jax
 import jax.numpy as jnp
 from jax import lax
+from jax.experimental import pallas as pl
+from jax.experimental.pallas import tpu as pltpu
 from jax.sharding import PartitionSpec as P
 
 HD = 64
@@ -83,6 +87,154 @@
 
 def token_sum(rows_in):
     return jnp.sum(rows_in.astype(jnp.float32), axis=0)
+
+
+def exchange_body(kind, chunks, *refs):
+    if kind == "forward":
+        partial, carry, gain, shift, carry_out, full, unit_out, inv_out = refs[:8]
+        scratch = refs[8:]
+    else:
+        partial, carry, gain, unit, inv, carry_out, full, gain_out, shift_out = refs[:9]
+        scratch = refs[9:]
+    from_pair, pair_sum, from_far = scratch[:3]
+    (near_s, near_r, far_s, far_r, gy_s, gy_r, gc_s, gc_r, fw_s, fw_r) = scratch[3:]
+    rows = carry.shape[0]
+    step = rows // chunks
+    me = lax.axis_index("col")
+    pair = me + 1 - 2 * (me % 2)
+    far = (me + 2) % 4
+    corner = (pair + 2) % 4
+
+    def at(block, chunk):
+        return pl.ds(pl.multiple_of(block * rows + chunk * step, step), step)
+
+    def send(src, dst, send_sem, recv_sem, target):
+        return pltpu.make_async_remote_copy(
+            src_ref=src,
+            dst_ref=dst,
+            send_sem=send_sem,
+            recv_sem=recv_sem,
+            device_id={"col": target},
+            device_id_type=pl.DeviceIdType.MESH,
+        )
+
+    barrier = pltpu.get_barrier_semaphore()
+    for other in (pair, far):
+        pl.semaphore_signal(
+            barrier, inc=1, device_id={"col": other}, device_id_type=pl.DeviceIdType.MESH
+        )
+    pl.semaphore_wait(barrier, 2)
+    near = []
+    for half, owner in enumerate((corner, pair)):
+        for chunk in range(chunks):
+            slot = half * chunks + chunk
+            copy = send(
+                partial.at[at(owner, chunk)],
+                from_pair.at[pl.ds(slot * step, step)],
+                near_s.at[slot],
+                near_r.at[slot],
+                pair,
+            )
+            copy.start()
+            near.append(copy)
+    over = []
+    for chunk in range(chunks):
+        near[chunk].wait_recv()
+        here = pl.ds(chunk * step, step)
+        pair_sum[here] = (
+            partial[at(far, chunk)].astype(jnp.float32) + from_pair[here].astype(jnp.float32)
+        ).astype(jnp.bfloat16)
+        copy = send(pair_sum.at[here], from_far.at[here], far_s.at[chunk], far_r.at[chunk], far)
+        copy.start()
+        over.append(copy)
+    if kind == "backward":
+        gain_sum = jnp.zeros((1, carry.shape[1]), jnp.float32)
+        shift_sum = jnp.zeros((1, carry.shape[1]), jnp.float32)
+    across = []
+    beside = []
+    for chunk in range(chunks):
+        near[chunks + chunk].wait_recv()
+        over[chunk].wait_recv()
+        here = pl.ds(chunk * step, step)
+        total = (
+            partial[at(me, chunk)].astype(jnp.float32)
+            + from_pair[pl.ds((chunks + chunk) * step, step)].astype(jnp.float32)
+            + from_far[here].astype(jnp.float32)
+        )
+        if kind == "forward":
+            value = carry[here] + total
+            carry_out[here] = value
+            unit_rows, inv_std = norm_unit(value)
+            unit_out[here] = unit_rows
+            inv_out[here] = jnp.broadcast_to(inv_std, (step, inv_out.shape[1]))
+            result = norm_apply(unit_rows, gain[...], shift[...])
+        else:
+            unit_rows = unit[here]
+            gain_sum = gain_sum + jnp.sum(total * unit_rows, axis=0, keepdims=True)
+            shift_sum = shift_sum + jnp.sum(total, axis=0, keepdims=True)
+            scaled = total * gain[...]
+            first = jnp.mean(scaled, axis=1, keepdims=True)
+            second = jnp.mean(scaled * unit_rows, axis=1, keepdims=True)
+            value = carry[here] + inv[here][:, :1] * (scaled - first - unit_rows * second)
+            carry_out[here] = value
+            result = value.astype(jnp.bfloat16)
+        mine = at(me, chunk)
+        full[mine] = result
+        copy = send(full.at[mine], full.at[mine], gy_s.at[chunk], gy_r.at[chunk], far)
+        copy.start()
+        across.append(copy)
+        copy = send(full.at[mine], full.at[mine], gc_s.at[chunk], gc_r.at[chunk], pair)
+        copy.start()
+        beside.append(copy)
+    if kind == "backward":
+        gain_out[...] = gain_sum
+        shift_out[...] = shift_sum
+    onward = []
+    for chunk in range(chunks):
+        across[chunk].wait_recv()
+        spot = at(far, chunk)
+        copy = send(full.at[spot], full.at[spot], fw_s.at[chunk], fw_r.at[chunk], pair)
+        copy.start()
+        onward.append(copy)
+    for copy in beside + onward:
+        copy.wait_recv()
+    for copy in near + over + across + beside + onward:
+        copy.wait_send()
+
+
+def exchange(kind, partial, carry, *rest):
+    rows, width = carry.shape
+    chunks = 4
+    wide = jax.ShapeDtypeStruct((rows, width), jnp.float32)
+    outs = [wide, jax.ShapeDtypeStruct((4 * rows, width), jnp.bfloat16)]
+    if kind == "forward":
+        outs += [wide, jax.ShapeDtypeStruct((rows, 128), jnp.float32)]
+    else:
+        outs += [jax.ShapeDtypeStruct((1, width), jnp.float32)] * 2
+    in_vmem = pl.BlockSpec(memory_space=pltpu.VMEM)
+    dma = pltpu.SemaphoreType.DMA
+    return pl.pallas_call(
+        functools.partial(exchange_body, kind, chunks),
+        out_shape=outs,
+        in_specs=[in_vmem] * (2 + len(rest)),
+        out_specs=[in_vmem] * len(outs),
+        scratch_shapes=[
+            pltpu.VMEM((2 * rows, width), jnp.bfloat16),
+            pltpu.VMEM((rows, width), jnp.bfloat16),
+            pltpu.VMEM((rows, width), jnp.bfloat16),
+        ]
+        + [dma((2 * chunks,))] * 2
+        + [dma((chunks,))] * 8,
+        cost_estimate=pl.CostEstimate(
+            flops=20 * rows * width, bytes_accessed=50_000_000, transcendentals=0
+        ),
+        compiler_params=pltpu.CompilerParams(
+            collective_id=1 if kind == "forward" else 2,
+            has_side_effects=True,
+            vmem_limit_bytes=32 * 1024 * 1024,
+        ),
+        name="exchange_" + kind,
+    )(partial, carry, *rest)
 
 
 def by_row(vector):
@@ -175,6 +327,11 @@
     x_full = lax.all_gather(inputs, "col", axis=0, tiled=True).T
     cot_full = lax.all_gather(cotangent, "col", axis=0, tiled=True).T
     resid = own_rows(x_full).astype(jnp.float32)
+    unit_one, inv_one = norm_unit(resid)
+    inv_one = jnp.broadcast_to(inv_one, (resid.shape[0], 128))
+    gain_of = [item.astype(jnp.float32)[None] for item in attention_gain]
+    shift_of = [item.astype(jnp.float32)[None] for item in attention_shift]
+    norm_one = norm_apply(norm_unit(x_full.astype(jnp.float32))[0], gain_of[0], shift_of[0])
     saved = []
     for layer_idx in range(layer_count):
         w_attn, w_feed = attn_w[layer_idx], feed_w[layer_idx]
@@ -185,15 +342,8 @@
         b_out = bias_of(layer_idx, 2 * small, small)
         b_contract = bias_of(layer_idx, 3 * small, small)
         b_expand = bias_of(layer_idx, 4 * small, hidden_part // row_count)
-        gain_one = attention_gain[layer_idx].astype(jnp.float32)
-        shift_one = attention_shift[layer_idx].astype(jnp.float32)
-        gain_two = feed_gain[layer_idx].astype(jnp.float32)
-        shift_two = feed_shift[layer_idx].astype(jnp.float32)
-        unit_one, inv_one = norm_unit(resid)
-        if layer_idx == 0:
-            norm_one = norm_apply(norm_unit(x_full.astype(jnp.float32))[0], gain_one, shift_one)
-        else:
-            norm_one = col_gather(norm_apply(unit_one, gain_one, shift_one))
+        gain_two = feed_gain[layer_idx].astype(jnp.float32)[None]
+        shift_two = feed_shift[layer_idx].astype(jnp.float32)[None]
         b_qkv = jnp.concatenate([b_query, jnp.zeros_like(b_query), b_value])
         qkv = (jnp.dot(norm_one, w_qkv, preferred_element_type=jnp.float32) + b_qkv).astype(
             jnp.bfloat16
@@ -204,14 +354,28 @@
             qkv[:, 2 * part :],
         )
         mixed_rows, log_totals = attend(query_rows, key_rows, value_rows)
-        resid = resid + col_scatter(contract_cols(mixed_rows, w_out) + spread_bias(b_out, width))
-        unit_two, inv_two = norm_unit(resid)
-        norm_two = col_gather(norm_apply(unit_two, gain_two, shift_two))
+        partial_rows = contract_cols(mixed_rows, w_out) + spread_bias(b_out, width)
+        resid, norm_two, unit_two, inv_two = exchange(
+            "forward", partial_rows.astype(jnp.bfloat16), resid, gain_two, shift_two
+        )
         before_act = jnp.dot(norm_two, w_expand, preferred_element_type=jnp.float32) + b_expand
         hidden_rows = gelu_tanh(before_act).astype(jnp.bfloat16)
         partial_rows = contract_cols(hidden_rows, w_contract) + spread_bias(b_contract, width)
+        saved.append(
+            (
+                (w_qkv, w_out, w_expand, w_contract, gain_two),
+                (norm_one, unit_one, inv_one, query_rows, key_rows, value_rows),
+                (mixed_rows, log_totals, norm_two, unit_two, inv_two, before_act, hidden_rows),
+            )
+        )
         if layer_idx + 1 < layer_count:
-            resid = resid + col_scatter(partial_rows)
+            resid, norm_one, unit_one, inv_one = exchange(
+                "forward",
+                partial_rows.astype(jnp.bfloat16),
+                resid,
+                gain_of[layer_idx + 1],
+                shift_of[layer_idx + 1],
+            )
         else:
             count = resid.shape[0]
             start = lax.axis_index("col") * count
@@ -220,13 +384,6 @@
             outputs = lax.psum_scatter(
                 partial_rows.astype(jnp.bfloat16), "col", scatter_dimension=1, tiled=True
             ).T
-        saved.append(
-            (
-                (w_qkv, w_out, w_expand, w_contract, gain_one, gain_two),
-                (norm_one, unit_one, inv_one, query_rows, key_rows, value_rows),
-                (mixed_rows, log_totals, norm_two, unit_two, inv_two, before_act, hidden_rows),
-            )
-        )
     grad = own_rows(cot_full).astype(jnp.float32)
     branch_full = cot_full
     packs = [None] * layer_count
@@ -234,19 +391,19 @@
     norm_sums = [None] * layer_count
     for layer_idx in reversed(range(layer_count)):
         (
-            (w_qkv, w_out, w_expand, w_contract, gain_one, gain_two),
+            (w_qkv, w_out, w_expand, w_contract, gain_two),
             (norm_one, unit_one, inv_one, query_rows, key_rows, value_rows),
             (mixed_rows, log_totals, norm_two, unit_two, inv_two, before_act, hidden_rows),
         ) = saved[layer_idx]
         d_hidden = jnp.dot(branch_full, w_contract, preferred_element_type=jnp.float32)
         d_before = jax.vjp(gelu_tanh, before_act)[1](d_hidden)[0].astype(jnp.bfloat16)
-        d_norm = col_scatter(contract_cols(d_before, w_expand))
+        d_partial = contract_cols(d_before, w_expand).astype(jnp.bfloat16)
         contract_part = contract_rows(branch_full, hidden_rows)
         expand_part = contract_rows(norm_two, d_before)
         contract_bias_part = token_sum(own_features(branch_full))
-        back_rows, gain_two_part, shift_two_part = norm_back(d_norm, unit_two, inv_two, gain_two)
-        grad = grad + back_rows
-        branch_full = col_gather(grad.astype(jnp.bfloat16))
+        grad, branch_full, gain_two_part, shift_two_part = exchange(
+            "backward", d_partial, grad, gain_two, unit_two, inv_two
+        )
         d_mixed = jnp.dot(branch_full, w_out, preferred_element_type=jnp.float32).astype(
             jnp.bfloat16
         )
@@ -254,11 +411,11 @@
         out_bias_part = token_sum(own_features(branch_full))
         d_query, d_key, d_value = attend_back(query_rows, key_rows, value_rows, log_totals, d_mixed)
         d_qkv = jnp.concatenate([d_query, d_key, d_value], axis=1)
-        d_norm = col_scatter(contract_cols(d_qkv, w_qkv))
+        d_partial = contract_cols(d_qkv, w_qkv).astype(jnp.bfloat16)
         qkv_part = contract_rows(norm_one, d_qkv)
-        back_rows, gain_one_part, shift_one_part = norm_back(d_norm, unit_one, inv_one, gain_one)
-        grad = grad + back_rows
-        branch_full = col_gather(grad.astype(jnp.bfloat16))
+        grad, branch_full, gain_one_part, shift_one_part = exchange(
+            "backward", d_partial, grad, gain_of[layer_idx], unit_one, inv_one
+        )
         packs[layer_idx] = jnp.concatenate([qkv_part, out_part, expand_part, contract_part], axis=1)
         vectors[layer_idx] = (
             token_sum(d_query),
@@ -267,7 +424,7 @@
             token_sum(d_before),
             contract_bias_part,
         )
-        norm_sums[layer_idx] = jnp.stack(
+        norm_sums[layer_idx] = jnp.concatenate(
             [gain_one_part, shift_one_part, gain_two_part, shift_two_part]
         )
     inputs_grad = own_features(branch_full).astype(jnp.float32).T

time: 905 us -> 575 us (0.64)
  waiting for transfers between devices: 608 us -> 213 us
  Pallas kernels: 0 us -> 163 us
  other arithmetic: 82.2 us -> 42.8 us
  local copies, waits for them, and re-layouts: 67.1 us -> 39.1 us
  matrix products: 106 us -> 79.3 us
    pallas_call x0 -> x7, Pallas kernels: none -> 163 us  [exchange(): pl.pallas_call(functools.partial(exchange_body, kind, chunks), out_shape=...]
    reduce_scatter x7 -> x0, waiting for transfers between devices: 146 us -> none  [col_scatter(): lax.psum_scatter(partial_rows.astype(jnp.bfloat16), 'col', scatter_dimens...]
    all_gather x7 -> x0, waiting for transfers between devices: 142 us -> none  [col_gather(): return lax.all_gather(rows_in, 'col', axis=0, tiled=True)]
    reduce_scatter x2, waiting for transfers between devices: 124 us -> 77.3 us  [row_total(): lax.psum_scatter(packed.astype(jnp.bfloat16), 'row', scatter_dimension=0,...]
    all_gather x1, waiting for transfers between devices: 44.7 us -> 9.67 us  [local(): feed_w = [lax.all_gather(feed_slabs[0], 'row', axis=0, tiled=True)]]
    all_gather x1, waiting for transfers between devices: 61.3 us -> 35.1 us  [local(): lax.all_gather(jnp.concatenate([attn_slab(layer_idx), feed_slabs[layer_id...]
    convert_element_type x7 -> x6, other arithmetic: 14.6 us -> 0.13 us  [the longest x1 0.05 us: local(): grad = own_rows(cot_full).astype(jnp.float32)]
    dot_general x8, matrix products: 28.4 us -> 16.7 us  [contract_cols(): lax.dot_general(left, right, (((1,), (1,)), ((), ())), preferred_element_...]
  transfers between devices with their start and end apart: 22 -> 8, of which waited for: 21 -> 7; matrix products, arithmetic and copies ran while one was open for 15% -> 20% of each run, Pallas kernels for 0% -> 21%
where the time goes in v2:
time: 575 us; the launch traced here: 564 us
  waiting for transfers between devices  213 us (37%)
  Pallas kernels  163 us (28%)
  matrix products  79.3 us (14%)
  other arithmetic  42.8 us (7%)
  local copies, waits for them, and re-layouts  39.1 us (7%)
  between operations  16.1 us (3%)
  blocking collectives  10.2 us (2%)
    pallas_call x7, Pallas kernels, exchange(): pl.pallas_call(functools.partial(exchange_body, kind, chunks), out_shape=...  163 us
    reduce_scatter x2, waiting for transfers between devices, row_total(): lax.psum_scatter(packed.astype(jnp.bfloat16), 'row', scatter_dimension=0,...  77.3 us
    all_gather x1, waiting for transfers between devices, local(): lax.all_gather(jnp.concatenate([attn_slab(0), bias_block], axis=0), 'row'...  35.8 us
    all_gather x1, waiting for transfers between devices, local(): lax.all_gather(jnp.concatenate([attn_slab(layer_idx), feed_slabs[layer_id...  35.1 us
    all_gather x1, waiting for transfers between devices, local(): cot_full = lax.all_gather(cotangent, 'col', axis=0, tiled=True).T  21.2 us
    transpose x1, waiting for transfers between devices, local(): outputs = lax.psum_scatter(partial_rows.astype(jnp.bfloat16), 'col', scat...  19.2 us
    unnamed x140, local copies, waits for them, and re-layouts  18.5 us
    dot_general x8, matrix products, contract_cols(): lax.dot_general(left, right, (((1,), (1,)), ((), ())), preferred_element_...  16.7 us
  transfers between devices with their start and end apart: 8, of which 7 were waited for; matrix products, arithmetic and copies ran while one was open for 20% of the time, Pallas kernels for 21%

profile of v2, /device:TPU:11, one launch (start us, length us, event | category | flops | bytes accessed | tf_op | source)
XLA Modules:
  0.0 564.1 jit_solution(6090022896241211832)
XLA Ops:
  12.4 1.2 slice_bitcast_fusion.44
  16.2 1.2 iota_compare_fusion
  17.4 13.5 %all-gather.7.cloned.1.call-done = bf16[768,1024]{1,0:T(8,128)(2,1)} async-done(((bf16[192,1024]{1,0:T(8,128)(2,1)}), bf16[768,1024]{1,0:T(8,128)(2,1)}) %all-gather.7.cloned.1.call-update) | async-done | bytes 1572880 | tf_op jit(solution)/shard_map/all_gather | solution.py:327
  30.9 21.2 %all-gather.13.cloned.1.call-done = bf16[768,1024]{1,0:T(8,128)(2,1)} async-done(((bf16[192,1024]{1,0:T(8,128)(2,1)}), bf16[768,1024]{1,0:T(8,128)(2,1)}) %all-gather.13.cloned.1.call-update) | async-done | bytes 1572880 | tf_op jit(solution)/shard_map/all_gather | solution.py:328
  52.1 1.2 constant_dynamic-slice_fusion
  53.7 1.8 convert_reduce_fusion
  59.3 35.8 %all-gather.15.cloned.1.call-done = bf16[896,768]{1,0:T(8,128)(2,1)} async-done(((bf16[112,768]{1,0:T(8,128)(2,1)}), bf16[896,768]{1,0:T(8,128)(2,1)}) %all-gather.15.cloned.1.call-update) | async-done | bytes 1376272 | tf_op jit(solution)/shard_map/all_gather | solution.py:298
  95.2 2.4 slice.413
  101.0 2.5 add_convert_fusion.4
  105.1 1.4 fusion.138
  106.5 1.5 fusion
  108.7 1.9 fusion.86
  110.6 1.9 add_convert_fusion.2.refs_0_
  112.6 23.7 %exchange_forward.3 = (f32[256,768]{1,0:T(8,128)S(1)}, bf16[1024,768]{1,0:T(8,128)(2,1)S(1)}, f32[256,768]{1,0:T(8,128)S(1)}, f32[256,128]{1,0:T(8,128)S(1)}) custom-call(bf16[1024,768]{1,0:T(8,128)(2,1)S(1)} %add_convert_fusion.2.refs_0_, f32[256,768]{1,0:T(8,128)S(1)} %convert_bitcast_fusion.1.refs_1_, f32[1,768]{1,0:T(1,128)S(1)} %get-tuple-element.197.refs_2_, ...), custom_call_target="tpu_custom_call" | custom-call | flops 3932160 | bytes 50000000 | tf_op jit(solution)/shard_map/exchange_forward/pallas_call | solution.py:216
  137.2 1.1 copy-done.11
  138.3 9.7 %all-gather.9.cloned.1.call-done = bf16[768,1536]{1,0:T(8,128)(2,1)} async-done(((bf16[96,1536]{1,0:T(8,128)(2,1)}), bf16[768,1536]{1,0:T(8,128)(2,1)}) %all-gather.9.cloned.1.call-update) | async-done | bytes 2359312 | tf_op jit(solution)/shard_map/all_gather | solution.py:313
  148.0 3.3 fusion.101
  151.3 2.1 add_convert_fusion.1.refs_0_
  153.5 24.1 %exchange_forward.4 = (f32[256,768]{1,0:T(8,128)S(1)}, bf16[1024,768]{1,0:T(8,128)(2,1)S(1)}, f32[256,768]{1,0:T(8,128)S(1)}, f32[256,128]{1,0:T(8,128)S(1)}) custom-call(bf16[1024,768]{1,0:T(8,128)(2,1)S(1)} %add_convert_fusion.1.refs_0_, f32[256,768]{1,0:T(8,128)S(1)} %get-tuple-element.45.refs_1_, f32[1,768]{1,0:T(1,128)S(1)} %get-tuple-element.193.refs_2_, ...), custom_call_target="tpu_custom_call" | custom-call | flops 3932160 | bytes 50000000 | tf_op jit(solution)/shard_map/exchange_forward/pallas_call | solution.py:216
  177.6 1.2 copy-done.13
  178.7 35.1 %all-gather.11.cloned.1.call-done = bf16[768,2304]{1,0:T(8,128)(2,1)} async-done(((bf16[96,2304]{1,0:T(8,128)(2,1)}), bf16[768,2304]{1,0:T(8,128)(2,1)}) %all-gather.11.cloned.1.call-update) | async-done | bytes 3538960 | tf_op jit(solution)/shard_map/all_gather | solution.py:315
  213.9 2.8 add_convert_fusion.3
  219.1 1.4 fusion.140
  220.6 1.4 fusion.1
  222.0 2.0 fusion.87
  224.8 24.3 %exchange_forward.5 = (f32[256,768]{1,0:T(8,128)S(1)}, bf16[1024,768]{1,0:T(8,128)(2,1)S(1)}, f32[256,768]{1,0:T(8,128)S(1)}, f32[256,128]{1,0:T(8,128)S(1)}) custom-call(bf16[1024,768]{1,0:T(8,128)(2,1)S(1)} %add_convert_fusion.refs_0_, f32[256,768]{1,0:T(8,128)S(1)} %get-tuple-element.47.refs_1_, f32[1,768]{1,0:T(1,128)S(1)} %get-tuple-element.196.refs_2_, ...), custom_call_target="tpu_custom_call" | custom-call | flops 3932160 | bytes 50000000 | tf_op jit(solution)/shard_map/exchange_forward/pallas_call | solution.py:216
  249.2 1.4 fusion.93
  250.8 4.4 fusion.145
  255.2 1.4 convolution_convert_fusion.5
  256.7 1.4 convolution_convert_fusion.3.refs_0_
  258.1 22.5 %exchange_backward.4 = (f32[256,768]{1,0:T(8,128)S(1)}, bf16[1024,768]{1,0:T(8,128)(2,1)S(1)}, f32[1,768]{1,0:T(1,128)S(1)}, f32[1,768]{1,0:T(1,128)S(1)}) custom-call(bf16[1024,768]{1,0:T(8,128)(2,1)S(1)} %convolution_convert_fusion.3.refs_0_, f32[256,768]{1,0:T(8,128)S(1)} %convert_bitcast_fusion.2.refs_1_, f32[1,768]{1,0:T(1,128)S(1)} %get-tuple-element.196.refs_2_, ...), custom_call_target="tpu_custom_call" | custom-call | flops 3932160 | bytes 50000000 | tf_op jit(solution)/shard_map/exchange_backward/pallas_call | solution.py:216
  285.1 2.0 multiply_reduce_fusion.1
  287.1 1.2 fusion.144
  288.4 1.3 multiply_convert_fusion.1
  293.4 2.3 fusion.45
  295.7 2.0 pad_maximum_fusion.2
  297.7 5.8 %copy.103 = bf16[768,2304]{1,0:T(8,128)(2,1)} copy(bf16[768,2304]{0,1:T(8,128)(2,1)} %pad_maximum_fusion.2) | data formatting | bytes 7077888
  303.6 3.2 convolution_convert_fusion.1.refs_0_
  306.8 22.5 %exchange_backward.5 = (f32[256,768]{1,0:T(8,128)S(1)}, bf16[1024,768]{1,0:T(8,128)(2,1)S(1)}, f32[1,768]{1,0:T(1,128)S(1)}, f32[1,768]{1,0:T(1,128)S(1)}) custom-call(bf16[1024,768]{1,0:T(8,128)(2,1)S(1)} %convolution_convert_fusion.1.refs_0_, f32[256,768]{1,0:T(8,128)S(1)} %copy-done.8, f32[1,768]{1,0:T(1,128)S(1)} %get-tuple-element.193.refs_2_, ...), custom_call_target="tpu_custom_call" | custom-call | flops 3932160 | bytes 50000000 | tf_op jit(solution)/shard_map/exchange_backward/pallas_call | solution.py:216
  329.3 4.4 fusion.143
  333.7 1.4 convolution_convert_fusion.2.refs_0_
  335.5 22.4 %exchange_backward.6 = (f32[256,768]{1,0:T(8,128)S(1)}, bf16[1024,768]{1,0:T(8,128)(2,1)S(1)}, f32[1,768]{1,0:T(1,128)S(1)}, f32[1,768]{1,0:T(1,128)S(1)}) custom-call(bf16[1024,768]{1,0:T(8,128)(2,1)S(1)} %convolution_convert_fusion.2.refs_0_, f32[256,768]{1,0:T(8,128)S(1)} %get-tuple-element.57.refs_1_, f32[1,768]{1,0:T(1,128)S(1)} %get-tuple-element.197.refs_2_, ...), custom_call_target="tpu_custom_call" | custom-call | flops 3932160 | bytes 50000000 | tf_op jit(solution)/shard_map/exchange_backward/pallas_call | solution.py:216
  358.8 1.8 convolution_convert_fusion.10
  360.6 1.4 fusion.70
  362.6 1.4 dynamic-slice_reduce_fusion.1
  364.5 4.9 fusion.142
  369.5 2.8 multiply_reduce_fusion.2
  372.4 3.0 multiply_convert_fusion.2
  375.8 1.9 multiply_reduce_fusion
  377.7 1.6 multiply_convert_fusion
  383.1 1.5 convolution_convert_fusion.7
  384.7 1.3 convolution_convert_fusion.9
  387.1 2.0 convolution_convert_fusion.6
  389.1 2.1 pad_maximum_fusion.1
  391.2 6.0 %copy.88 = bf16[768,2304]{1,0:T(8,128)(2,1)} copy(bf16[768,2304]{0,1:T(8,128)(2,1)} %pad_maximum_fusion.1) | data formatting | bytes 7077888 | tf_op jit(solution)/shard_map/concatenate | solution.py:419
  397.3 1.5 convolution_convert_fusion.refs_0_
  398.9 23.4 %exchange_backward.7 = (f32[256,768]{1,0:T(8,128)}, bf16[1024,768]{1,0:T(8,128)(2,1)S(1)}, f32[1,768]{1,0:T(1,128)S(1)}, f32[1,768]{1,0:T(1,128)S(1)}) custom-call(bf16[1024,768]{1,0:T(8,128)(2,1)S(1)} %convolution_convert_fusion.refs_0_, f32[256,768]{1,0:T(8,128)S(1)} %copy-done.6, f32[1,768]{1,0:T(1,128)S(1)} %get-tuple-element.192.refs_2_, ...), custom_call_target="tpu_custom_call" | custom-call | flops 3932160 | bytes 50000000 | tf_op jit(solution)/shard_map/exchange_backward/pallas_call | solution.py:216
  422.4 10.2 %psum.7 = bf16[2,4,768]{2,1,0:T(4,128)(2,1)S(1)} all-reduce(f32[2,4,768]{2,1,0:T(4,128)S(1)} %pad_maximum_fusion.19), channel_id=1, replica_groups=mesh['row'=8,'col'=4] {'col'}, use_global_device_ids=true, to_apply=%region_22.23 | all-reduce | flops 6144 | bytes 36864 | tf_op jit(solution)/shard_map/psum | solution.py:431
  433.7 4.2 pad_maximum_fusion
  439.2 4.4 convolution_add_fusion
  443.9 1.7 copy.101
  445.8 1.2 copy.91
  448.3 77.3 %reduce-scatter.8.cloned.1.call-done = bf16[1,112,2304]{2,1,0:T(8,128)(2,1)} async-done(((bf16[8,112,2304]{2,1,0:T(8,128)(2,1)}), bf16[1,112,2304]{2,1,0:T(8,128)(2,1)}) %reduce-scatter.8.cloned.1.call-update) | async-done | bytes 516112 | tf_op jit(solution)/shard_map/reduce_scatter | solution.py:245
  537.6 19.2 %reduce-scatter.10.cloned.1.call-done = bf16[192,1024]{1,0:T(8,128)(2,1)} async-done(((bf16[768,1024]{1,0:T(8,128)(2,1)}), bf16[192,1024]{1,0:T(8,128)(2,1)}) %reduce-scatter.10.cloned.1.call-update) | async-done | bytes 393232 | tf_op jit(solution)/shard_map/transpose | solution.py:386
  (293 shorter events, 53.8 us)
Async XLA Ops:
  7.2 8.1 %copy-start.50 = (bf16[2,768]{1,0:T(2,128)(2,1)S(1)}, bf16[2,768]{1,0:T(2,128)(2,1)}, u32[]{:S(2)}) copy-start(bf16[2,768]{1,0:T(2,128)(2,1)} %param.27) | copy-start | bytes 9220
  7.2 8.1 %copy-start.48 = (bf16[2,768]{1,0:T(2,128)(2,1)S(1)}, bf16[2,768]{1,0:T(2,128)(2,1)}, u32[]{:S(2)}) copy-start(bf16[2,768]{1,0:T(2,128)(2,1)} %param.26) | copy-start | bytes 9220
  7.2 9.0 %copy-start.51 = (bf16[2,768]{1,0:T(2,128)(2,1)S(1)}, bf16[2,768]{1,0:T(2,128)(2,1)}, u32[]{:S(2)}) copy-start(bf16[2,768]{1,0:T(2,128)(2,1)} %param.32) | copy-start | bytes 9220
  7.2 9.0 %copy-start.52 = (bf16[2,768]{1,0:T(2,128)(2,1)S(1)}, bf16[2,768]{1,0:T(2,128)(2,1)}, u32[]{:S(2)}) copy-start(bf16[2,768]{1,0:T(2,128)(2,1)} %param.33) | copy-start | bytes 9220
  7.2 23.6 %all-gather.7.cloned.1.call-start = ((), (), s32[]{:S(2)}) async-start(), calls=%async_computation.3 | async-start | bytes 1966080 | tf_op jit(solution)/shard_map/all_gather | solution.py:327
  8.0 44.1 %all-gather.13.cloned.1.call-start = ((), (), s32[]{:S(2)}) async-start(), calls=%async_computation.6 | async-start | bytes 1966080 | tf_op jit(solution)/shard_map/all_gather | solution.py:328
  8.7 86.5 %all-gather.15.cloned.1.call-start = ((), (), s32[]{:S(2)}) async-start(), calls=%async_computation.8 | async-start | bytes 1548288 | tf_op jit(solution)/shard_map/all_gather | solution.py:298
  12.3 135.7 %all-gather.9.cloned.1.call-start = ((), (), s32[]{:S(2)}) async-start(), calls=%async_computation.4 | async-start | bytes 2654208 | tf_op jit(solution)/shard_map/all_gather | solution.py:313
  14.3 199.6 %all-gather.11.cloned.1.call-start = ((), (), s32[]{:S(2)}) async-start(), calls=%async_computation.5 | async-start | bytes 3981312 | tf_op jit(solution)/shard_map/all_gather | solution.py:315
  15.2 431.8 %reduce-scatter.12.cloned.1.call-start = ((), (), s32[]{:S(2)}) async-start(), calls=%async_computation.10 | async-start | bytes 3981312 | tf_op jit(solution)/shard_map/reduce_scatter | solution.py:245
  53.5 2.0 copy-start.18
  56.4 42.2 %copy-start.53 = (f32[256]{0:T(256)}, f32[256]{0:T(256)S(1)}, u32[]{:S(2)}) copy-start(f32[256]{0:T(256)S(1)} %add_rsqrt_fusion.1) | copy-start | bytes 3076
  59.3 41.6 %copy-start.19 = (bf16[768,1024]{1,0:T(8,128)(2,1)S(1)}, bf16[768,1024]{1,0:T(8,128)(2,1)}, u32[]{:S(2)}) copy-start(bf16[768,1024]{1,0:T(8,128)(2,1)} %all-gather.7.cloned.1.call-done) | copy-start | bytes 4718596
  101.0 2.7 copy-start.45
  103.6 5.0 copy-start.28
  103.6 1.4 copy-start.23
  104.4 4.2 copy-start.16
  106.5 4.1 copy-start.15
  110.6 2.0 copy-start.34
  148.0 3.3 copy-start.56
  151.3 2.2 copy-start.59
  213.9 2.9 copy-start.46
  222.0 2.0 copy-start.47
  249.1 1.4 copy-start.1
  249.1 1.7 copy-start.41
  250.8 42.5 %copy-start.58 = (f32[1024,768]{1,0:T(8,128)}, f32[1024,768]{1,0:T(8,128)S(1)}, u32[]{:S(2)}) copy-start(f32[1024,768]{1,0:T(8,128)S(1)} %fusion.93) | copy-start | bytes 9437188
  280.6 1.9 copy-start.7
  288.4 3.3 copy-start.37
  290.8 1.4 copy-start.14
  291.5 1.8 copy-start.42
  291.6 1.7 copy-start.40
  303.5 3.2 copy-start.8
  303.5 222.1 %reduce-scatter.8.cloned.1.call-start = ((), (), s32[]{:S(2)}) async-start(), calls=%async_computation.7 | async-start | bytes 4644864 | tf_op jit(solution)/shard_map/reduce_scatter | solution.py:245
  303.6 25.7 %copy-start.60 = (f32[1024,768]{1,0:T(8,128)S(1)}, f32[1024,768]{1,0:T(8,128)}, u32[]{:S(2)}) copy-start(f32[1024,768]{1,0:T(8,128)} %copy-done.59) | copy-start | bytes 9437188
  306.8 22.6 %copy-start.57 = (bf16[768,1536]{1,0:T(8,128)(2,1)S(1)}, bf16[768,1536]{1,0:T(8,128)(2,1)}, u32[]{:S(2)}) copy-start(bf16[768,1536]{1,0:T(8,128)(2,1)} %all-gather.9.cloned.1.call-done) | copy-start | bytes 7077892
  329.3 4.4 copy-start.9
  333.7 1.5 copy-start.62
  333.7 1.7 copy-start.4
  335.2 25.4 %copy-start.17 = (f32[3,512,512]{1,2,0:T(8,128)S(1)}, f32[3,512,512]{1,2,0:T(8,128)}, u32[]{:S(2)}) copy-start(f32[3,512,512]{1,2,0:T(8,128)} %copy-done.16) | copy-start | bytes 9437188
  364.5 5.0 copy-start.26
  364.5 5.0 copy-start.29
  369.5 6.2 %slice-start = ((s8[6291456]{0:T(1024)(128)(4,1)}), s8[4194304]{0:T(1024)(128)(4,1)S(1)}, s32[]{:S(2)}) async-start(s8[6291456]{0:T(1024)(128)(4,1)} %bitcast.350), calls=%async_computation.11 | async-start | bytes 8388608
  372.3 3.0 copy-start.22
  372.3 3.4 slice-start.1
  372.3 3.4 copy-start.27
  372.4 3.4 copy-start.30
  379.4 1.8 copy-start.35
  380.6 4.0 copy-start.38
  381.2 1.4 copy-start.12
  381.2 1.9 copy-start.63
  383.1 1.5 copy-start.43
  383.1 1.5 copy-start.20
  383.1 1.6 copy-start.36
  384.7 1.4 copy-start.10
  384.7 2.4 copy-start.61
  391.2 6.1 %copy-start.33 = (bf16[8,96,768]{2,1,0:T(8,128)(2,1)S(1)}, bf16[8,96,768]{2,1,0:T(8,128)(2,1)}, u32[]{:S(2)}) copy-start(bf16[8,96,768]{2,1,0:T(8,128)(2,1)} %slice.413) | copy-start | bytes 3538948
  391.2 6.1 %copy-start.39 = (bf16[1,1024,3,64]{1,3,2,0:T(8,128)(2,1)S(1)}, bf16[1,1024,3,64]{1,3,2,0:T(8,128)(2,1)}, u32[]{:S(2)}) copy-start(bf16[1,1024,3,64]{1,3,2,0:T(8,128)(2,1)} %copy-done.38) | copy-start | bytes 1179652
  391.2 6.1 %copy-start.44 = (bf16[1,1024,3,64]{1,3,2,0:T(8,128)(2,1)S(1)}, bf16[1,1024,3,64]{1,3,2,0:T(8,128)(2,1)}, u32[]{:S(2)}) copy-start(bf16[1,1024,3,64]{1,3,2,0:T(8,128)(2,1)} %copy-done.43) | copy-start | bytes 1179652
  397.3 1.5 copy-start.54
  397.3 1.6 copy-start
  397.3 1.6 copy-start.6
  398.8 34.6 %copy-start.55 = (bf16[8,24]{1,0:T(8,128)(2,1)S(1)}, bf16[8,24]{1,0:T(8,128)(2,1)}, u32[]{:S(2)}) copy-start(bf16[8,24]{1,0:T(8,128)(2,1)} %reshape.696) | copy-start | bytes 1156
  437.9 118.9 %reduce-scatter.10.cloned.1.call-start = ((), (), s32[]{:S(2)}) async-start(), calls=%async_computation.9 | async-start | bytes 1966080 | tf_op jit(solution)/shard_map/transpose | solution.py:386
  439.2 4.4 copy-start.2
  (10 other events, 11.0 us)
Sparse Core Ops, SparseCore 0:
  9.6 21.1 all-gather.6
  32.4 19.6 all-gather.12
  54.9 40.2 all-gather.14
  97.8 50.1 all-gather.8
  150.6 63.2 all-gather.10
  303.6 77.9 reduce-scatter.11
  438.0 87.5 reduce-scatter.7
  528.9 27.8 reduce-scatter.9

commit v3 on v2

--- a/solution.py
+++ b/solution.py
@@ -94,8 +94,8 @@
         partial, carry, gain, shift, carry_out, full, unit_out, inv_out = refs[:8]
         scratch = refs[8:]
     else:
-        partial, carry, gain, unit, inv, carry_out, full, gain_out, shift_out = refs[:9]
-        scratch = refs[9:]
+        partial, carry, gain, unit, inv, carry_out, full, sums_out = refs[:8]
+        scratch, (sums, sums_s, sums_r) = refs[8:-3], refs[-3:]
     from_pair, pair_sum, from_far = scratch[:3]
     (near_s, near_r, far_s, far_r, gy_s, gy_r, gc_s, gc_r, fw_s, fw_r) = scratch[3:]
     rows = carry.shape[0]
@@ -119,11 +119,12 @@
         )
 
     barrier = pltpu.get_barrier_semaphore()
-    for other in (pair, far):
+    greeted = (pair, far) if kind == "forward" else (pair, far, corner)
+    for other in greeted:
         pl.semaphore_signal(
             barrier, inc=1, device_id={"col": other}, device_id_type=pl.DeviceIdType.MESH
         )
-    pl.semaphore_wait(barrier, 2)
+    pl.semaphore_wait(barrier, len(greeted))
     near = []
     for half, owner in enumerate((corner, pair)):
         for chunk in range(chunks):
@@ -187,8 +188,14 @@
         copy.start()
         beside.append(copy)
     if kind == "backward":
-        gain_out[...] = gain_sum
-        shift_out[...] = shift_sum
+        sums[me] = jnp.concatenate(
+            [gain_sum, shift_sum, jnp.zeros((6, gain_sum.shape[1]), jnp.float32)], axis=0
+        )
+        small = []
+        for slot, other in enumerate(greeted):
+            copy = send(sums.at[me], sums.at[me], sums_s.at[slot], sums_r.at[slot], other)
+            copy.start()
+            small.append(copy)
     onward = []
     for chunk in range(chunks):
         across[chunk].wait_recv()
@@ -198,6 +205,11 @@
         onward.append(copy)
     for copy in beside + onward:
         copy.wait_recv()
+    if kind == "backward":
+        for copy in small:
+            copy.wait_recv()
+        sums_out[...] = sums[0] + sums[1] + sums[2] + sums[3]
+        onward = onward + small
     for copy in near + over + across + beside + onward:
         copy.wait_send()
 
@@ -210,7 +222,7 @@
     if kind == "forward":
         outs += [wide, jax.ShapeDtypeStruct((rows, 128), jnp.float32)]
     else:
-        outs += [jax.ShapeDtypeStruct((1, width), jnp.float32)] * 2
+        outs += [jax.ShapeDtypeStruct((8, width), jnp.float32)]
     in_vmem = pl.BlockSpec(memory_space=pltpu.VMEM)
     dma = pltpu.SemaphoreType.DMA
     return pl.pallas_call(
@@ -224,7 +236,12 @@
             pltpu.VMEM((rows, width), jnp.bfloat16),
         ]
         + [dma((2 * chunks,))] * 2
-        + [dma((chunks,))] * 8,
+        + [dma((chunks,))] * 8
+        + (
+            []
+            if kind == "forward"
+            else [pltpu.VMEM((4, 8, width), jnp.float32), dma((3,)), dma((3,))]
+        ),
         cost_estimate=pl.CostEstimate(
             flops=20 * rows * width, bytes_accessed=50_000_000, transcendentals=0
         ),
@@ -235,6 +252,152 @@
         ),
         name="exchange_" + kind,
     )(partial, carry, *rest)
+
+
+def gather_body(chunks, block, full, gy_s, gy_r, gc_s, gc_r, fw_s, fw_r):
+    rows = block.shape[0]
+    step = rows // chunks
+    me = lax.axis_index("col")
+    pair = me + 1 - 2 * (me % 2)
+    far = (me + 2) % 4
+
+    def at(owner, chunk):
+        return pl.ds(pl.multiple_of(owner * rows + chunk * step, step), step)
+
+    def send(src, dst, send_sem, recv_sem, target):
+        return pltpu.make_async_remote_copy(
+            src_ref=src,
+            dst_ref=dst,
+            send_sem=send_sem,
+            recv_sem=recv_sem,
+            device_id={"col": target},
+            device_id_type=pl.DeviceIdType.MESH,
+        )
+
+    barrier = pltpu.get_barrier_semaphore()
+    for other in (pair, far):
+        pl.semaphore_signal(
+            barrier, inc=1, device_id={"col": other}, device_id_type=pl.DeviceIdType.MESH
+        )
+    pl.semaphore_wait(barrier, 2)
+    across, beside, onward = [], [], []
+    for chunk in range(chunks):
+        here = block.at[pl.ds(chunk * step, step)]
+        mine = full.at[at(me, chunk)]
+        across.append(send(here, mine, gy_s.at[chunk], gy_r.at[chunk], far))
+        across[-1].start()
+        beside.append(send(here, mine, gc_s.at[chunk], gc_r.at[chunk], pair))
+        beside[-1].start()
+    full[pl.ds(pl.multiple_of(me * rows, rows), rows)] = block[...]
+    for chunk in range(chunks):
+        across[chunk].wait_recv()
+        spot = full.at[at(far, chunk)]
+        onward.append(send(spot, spot, fw_s.at[chunk], fw_r.at[chunk], pair))
+        onward[-1].start()
+    for copy in beside + onward:
+        copy.wait_recv()
+    for copy in across + beside + onward:
+        copy.wait_send()
+
+
+def first_gather(block):
+    chunks = 4
+    rows, width = block.shape
+    in_vmem = pl.BlockSpec(memory_space=pltpu.VMEM)
+    return pl.pallas_call(
+        functools.partial(gather_body, chunks),
+        out_shape=jax.ShapeDtypeStruct((4 * rows, width), block.dtype),
+        in_specs=[in_vmem],
+        out_specs=in_vmem,
+        scratch_shapes=[pltpu.SemaphoreType.DMA((chunks,))] * 6,
+        cost_estimate=pl.CostEstimate(flops=0, bytes_accessed=30_000_000, transcendentals=0),
+        compiler_params=pltpu.CompilerParams(
+            collective_id=3, has_side_effects=True, vmem_limit_bytes=32 * 1024 * 1024
+        ),
+        name="first_gather",
+    )(block)
+
+
+def row_sum_body(count, weights, loose, weights_out, loose_out, packed, landed, send_sem, recv_sem):
+    slab = weights.shape[1]
+    head = loose.shape[1]
+    me = lax.axis_index("row")
+
+    def copy_to(offset):
+        target = (me + offset) % count
+        return pltpu.make_async_remote_copy(
+            src_ref=packed.at[offset],
+            dst_ref=landed.at[offset],
+            send_sem=send_sem.at[offset],
+            recv_sem=recv_sem.at[offset],
+            device_id={"row": target},
+            device_id_type=pl.DeviceIdType.MESH,
+        )
+
+    barrier = pltpu.get_barrier_semaphore()
+
+    def greet(offset, carry):
+        pl.semaphore_signal(
+            barrier,
+            inc=1,
+            device_id={"row": (me + offset) % count},
+            device_id_type=pl.DeviceIdType.MESH,
+        )
+        return carry
+
+    lax.fori_loop(1, count, greet, 0)
+    pl.semaphore_wait(barrier, count - 1)
+
+    def launch(offset, carry):
+        target = (me + offset) % count
+        packed[offset, :head] = loose[target].astype(jnp.bfloat16)
+        packed[offset, head : head + slab] = weights[target].astype(jnp.bfloat16)
+        if packed.shape[1] > head + slab:
+            packed[offset, head + slab :] = jnp.zeros(
+                (packed.shape[1] - head - slab, packed.shape[2]), jnp.bfloat16
+            )
+        copy_to(offset).start()
+        return carry
+
+    lax.fori_loop(1, count, launch, 0)
+    weights_out[...] = weights[me]
+    loose_out[...] = loose[me]
+
+    def collect(offset, carry):
+        copy_to(offset).wait_recv()
+        loose_out[...] += landed[offset, :head].astype(jnp.float32)
+        weights_out[...] += landed[offset, head : head + slab].astype(jnp.float32)
+        copy_to(offset).wait_send()
+        return carry
+
+    lax.fori_loop(1, count, collect, 0)
+
+
+def row_sum(weights, loose):
+    count, slab, width = weights.shape
+    head = loose.shape[1]
+    block = -(-(head + slab) // 16) * 16
+    in_vmem = pl.BlockSpec(memory_space=pltpu.VMEM)
+    return pl.pallas_call(
+        functools.partial(row_sum_body, count),
+        out_shape=[
+            jax.ShapeDtypeStruct((slab, width), jnp.float32),
+            jax.ShapeDtypeStruct((head, width), jnp.float32),
+        ],
+        in_specs=[in_vmem] * 2,
+        out_specs=[in_vmem] * 2,
+        scratch_shapes=[
+            pltpu.VMEM((count, block, width), jnp.bfloat16),
+            pltpu.VMEM((count, block, width), jnp.bfloat16),
+            pltpu.SemaphoreType.DMA((count,)),
+            pltpu.SemaphoreType.DMA((count,)),
+        ],
+        cost_estimate=pl.CostEstimate(flops=0, bytes_accessed=80_000_000, transcendentals=0),
+        compiler_params=pltpu.CompilerParams(
+            collective_id=4, has_side_effects=True, vmem_limit_bytes=40 * 1024 * 1024
+        ),
+        name="row_sum",
+    )(weights, loose)
 
 
 def by_row(vector):
@@ -302,9 +465,6 @@
         first_pack[:, slab:].reshape(row_count, -1)[:, :bias_len].reshape(row_count, layer_count, -1)
     )
     small = part // row_count
-    rest = [("feed", 0)]
-    for layer_idx in range(1, layer_count):
-        rest += [("attn", layer_idx), ("feed", layer_idx)]
     feed_slabs = [
         jnp.concatenate([expand_weight[item], contract_weight[item]], axis=1)
         for item in range(layer_count)
@@ -312,20 +472,13 @@
     attn_w = [first_pack[:, :slab].reshape(width, attn_width)]
     feed_w = [lax.all_gather(feed_slabs[0], "row", axis=0, tiled=True)]
     for layer_idx in range(1, layer_count):
-        both = lax.all_gather(
-            jnp.concatenate([attn_slab(layer_idx), feed_slabs[layer_idx]], axis=1),
-            "row",
-            axis=0,
-            tiled=True,
-        )
-        attn_w.append(both[:, :attn_width])
-        feed_w.append(both[:, attn_width:])
+        attn_w.append(lax.all_gather(attn_slab(layer_idx), "row", axis=0, tiled=True))
+        feed_w.append(lax.all_gather(feed_slabs[layer_idx], "row", axis=0, tiled=True))
 
     def bias_of(layer_idx, start, count):
         return gathered_bias[:, layer_idx, start : start + count].reshape(-1)
 
-    x_full = lax.all_gather(inputs, "col", axis=0, tiled=True).T
-    cot_full = lax.all_gather(cotangent, "col", axis=0, tiled=True).T
+    x_full = first_gather(inputs).T
     resid = own_rows(x_full).astype(jnp.float32)
     unit_one, inv_one = norm_unit(resid)
     inv_one = jnp.broadcast_to(inv_one, (resid.shape[0], 128))
@@ -358,6 +511,9 @@
         resid, norm_two, unit_two, inv_two = exchange(
             "forward", partial_rows.astype(jnp.bfloat16), resid, gain_two, shift_two
         )
+        if layer_idx == 0:
+            held, norm_two = lax.optimization_barrier((cotangent, norm_two))
+            cot_full = lax.all_gather(held, "col", axis=0, tiled=True).T
         before_act = jnp.dot(norm_two, w_expand, preferred_element_type=jnp.float32) + b_expand
         hidden_rows = gelu_tanh(before_act).astype(jnp.bfloat16)
         partial_rows = contract_cols(hidden_rows, w_contract) + spread_bias(b_contract, width)
@@ -401,7 +557,7 @@
         contract_part = contract_rows(branch_full, hidden_rows)
         expand_part = contract_rows(norm_two, d_before)
         contract_bias_part = token_sum(own_features(branch_full))
-        grad, branch_full, gain_two_part, shift_two_part = exchange(
+        grad, branch_full, two_sums = exchange(
             "backward", d_partial, grad, gain_two, unit_two, inv_two
         )
         d_mixed = jnp.dot(branch_full, w_out, preferred_element_type=jnp.float32).astype(
@@ -412,11 +568,13 @@
         d_query, d_key, d_value = attend_back(query_rows, key_rows, value_rows, log_totals, d_mixed)
         d_qkv = jnp.concatenate([d_query, d_key, d_value], axis=1)
         d_partial = contract_cols(d_qkv, w_qkv).astype(jnp.bfloat16)
+        if layer_idx + 1 == layer_count:
+            outputs, d_partial = lax.optimization_barrier((outputs, d_partial))
         qkv_part = contract_rows(norm_one, d_qkv)
-        grad, branch_full, gain_one_part, shift_one_part = exchange(
+        grad, branch_full, one_sums = exchange(
             "backward", d_partial, grad, gain_of[layer_idx], unit_one, inv_one
         )
-        packs[layer_idx] = jnp.concatenate([qkv_part, out_part, expand_part, contract_part], axis=1)
+        packs[layer_idx] = (qkv_part, out_part, expand_part, contract_part)
         vectors[layer_idx] = (
             token_sum(d_query),
             token_sum(d_value),
@@ -425,29 +583,47 @@
             contract_bias_part,
         )
         norm_sums[layer_idx] = jnp.concatenate(
-            [gain_one_part, shift_one_part, gain_two_part, shift_two_part]
+            [one_sums[:2], two_sums[:2]]
         )
     inputs_grad = own_features(branch_full).astype(jnp.float32).T
-    norm_total = own_features(lax.psum(jnp.stack(norm_sums), "col"))
+    norm_total = own_features(jnp.stack(norm_sums))
     flat = []
     for layer_idx in range(layer_count):
         flat += [by_row(item) for item in vectors[layer_idx]]
         flat += [by_row(norm_total[layer_idx, item]) for item in range(4)]
     sizes = [item.shape[1] for item in flat]
     flat = jnp.concatenate(flat, axis=1)
-    pack_width = packs[0].shape[1]
-    extra = -(-flat.shape[1] // (pack_width * 16)) * 16
-    flat = jnp.pad(flat, ((0, 0), (0, extra * pack_width - flat.shape[1])))
-    last_pack = jnp.concatenate(
-        [
-            packs[0].reshape(row_count, slab, pack_width),
-            flat.reshape(row_count, extra, pack_width),
-        ],
-        axis=1,
-    )
-    last_total = row_total(last_pack)[0]
-    totals = [last_total[:slab]] + [row_total(packs[item]) for item in range(1, layer_count)]
-    loose = last_total[slab:].reshape(-1)
+    qkv_width = 3 * part
+    head = -(-flat.shape[1] // (qkv_width * 16)) * 16
+    flat = jnp.pad(flat, ((0, 0), (0, head * qkv_width - flat.shape[1])))
+    qkv_total, loose = row_sum(
+        packs[0][0].reshape(row_count, slab, qkv_width), flat.reshape(row_count, head, qkv_width)
+    )
+    loose = loose.reshape(-1)
+    last = layer_count - 1
+    feed_total = row_total(jnp.concatenate(packs[last][2:], axis=1))
+    others = []
+    for layer_idx in range(layer_count):
+        others.append(packs[layer_idx][1])
+        if layer_idx > 0:
+            others.append(packs[layer_idx][0])
+        if layer_idx < last:
+            others += packs[layer_idx][2:]
+    joined = row_total(jnp.concatenate(others, axis=1))
+    totals = []
+    start = 0
+    for layer_idx in range(layer_count):
+        out_total = joined[:, start : start + part]
+        start += part
+        if layer_idx > 0:
+            qkv_total = joined[:, start : start + qkv_width]
+            start += qkv_width
+        if layer_idx < last:
+            feed_now = joined[:, start : start + 2 * hidden_part]
+            start += 2 * hidden_part
+        else:
+            feed_now = feed_total
+        totals.append(jnp.concatenate([qkv_total, out_total, feed_now], axis=1))
     pieces = []
     start = 0
     for size in sizes:

time: 575 us -> 513 us (0.89); the launches traced: 564 us -> 508 us
  waiting for transfers between devices: 213 us -> 75.3 us
  Pallas kernels: 163 us -> 227 us
  matrix products: 79.3 us -> 99 us
  local copies, waits for them, and re-layouts: 39.1 us -> 51.6 us
  blocking collectives: 10.2 us -> 0 us
    reduce_scatter x2, waiting for transfers between devices: 77.3 us -> 0.04 us  [row_total(): lax.psum_scatter(packed.astype(jnp.bfloat16), 'row', scatter_dimension=0,...]
    pallas_call x0 -> x2, Pallas kernels: none -> 54.5 us  [the longest x1 41.5 us: row_sum(): pl.pallas_call(functools.partial(row_sum_body, count), out_shape=[jax.Sha...]
    all_gather x3, waiting for transfers between devices: 69.9 us -> 43.1 us  [the longest x1 16.9 us: local(): lax.all_gather(feed_slabs[layer_idx], 'row', axis=0, tiled=True)]
    transpose x1 -> x0, waiting for transfers between devices: 19.2 us -> none  [local(): outputs = lax.psum_scatter(partial_rows.astype(jnp.bfloat16), 'col', scat...]
    all_gather x1, waiting for transfers between devices: 35.8 us -> 21.5 us  [local(): lax.all_gather(jnp.concatenate([attn_slab(0), bias_block], axis=0), 'row'...]
    psum x1 -> x0, blocking collectives: 10.2 us -> none  [local(): norm_total = own_features(lax.psum(jnp.stack(norm_sums), 'col'))]
    pallas_call x7, Pallas kernels: 163 us -> 173 us  [exchange(): pl.pallas_call(functools.partial(exchange_body, kind, chunks), out_shape=...]
    dot_general x4, matrix products: 7.5 us -> 13.5 us  [attend_back(): jnp.einsum('sqhd,skhd->shqk', grad_block, value_seq[:, :row_end], preferr...]
  transfers between devices with their start and end apart: 8 -> 8, of which waited for: 7 -> 5; matrix products, arithmetic and copies ran while one was open for 20% -> 33% of each run, Pallas kernels for 21% -> 45%
where the time goes in v3:
time: 513 us; the launch traced here: 508 us
  Pallas kernels  227 us (44%)
  matrix products  99 us (19%)
  waiting for transfers between devices  75.3 us (15%)
  local copies, waits for them, and re-layouts  51.6 us (10%)
  other arithmetic  37.7 us (7%)
  between operations  16.3 us (3%)
    pallas_call x7, Pallas kernels, exchange(): pl.pallas_call(functools.partial(exchange_body, kind, chunks), out_shape=...  173 us
    pallas_call x1, Pallas kernels, row_sum(): pl.pallas_call(functools.partial(row_sum_body, count), out_shape=[jax.Sha...  41.5 us
    all_gather x1, waiting for transfers between devices, local(): lax.all_gather(jnp.concatenate([attn_slab(0), bias_block], axis=0), 'row'...  21.5 us
    unnamed x214, local copies, waits for them, and re-layouts  20.3 us
    all_gather x1, waiting for transfers between devices, local(): lax.all_gather(feed_slabs[layer_idx], 'row', axis=0, tiled=True)  16.9 us
    dot_general x8, matrix products, contract_rows(): lax.dot_general(left, right, (((0,), (0,)), ((), ())), preferred_element_...  15.8 us
    dot_general x8, matrix products, contract_cols(): lax.dot_general(left, right, (((1,), (1,)), ((), ())), preferred_element_...  15.3 us
    all_gather x1, waiting for transfers between devices, local(): cot_full = lax.all_gather(held, 'col', axis=0, tiled=True).T  14.1 us
  transfers between devices with their start and end apart: 8, of which 5 were waited for; matrix products, arithmetic and copies ran while one was open for 33% of the time, Pallas kernels for 45%

profile of v3, /device:TPU:11, one launch (start us, length us, event | category | flops | bytes accessed | tf_op | source)
XLA Modules:
  0.0 508.0 jit_solution(10580439190559113316)
XLA Ops:
  10.9 1.2 slice_bitcast_fusion.43
  15.4 13.0 %first_gather.1 = bf16[768,1024]{1,0:T(8,128)(2,1)S(1)} custom-call(bf16[192,1024]{1,0:T(8,128)(2,1)S(1)} %copy-done.11), custom_call_target="tpu_custom_call" | custom-call | bytes 30000000 | tf_op jit(solution)/shard_map/first_gather/pallas_call | solution.py:307
  31.5 21.5 %all-gather.15.cloned.1.call-done = bf16[896,768]{1,0:T(8,128)(2,1)} async-done(((bf16[112,768]{1,0:T(8,128)(2,1)}), bf16[896,768]{1,0:T(8,128)(2,1)}) %all-gather.15.cloned.1.call-update) | async-done | bytes 1376272 | tf_op jit(solution)/shard_map/all_gather | solution.py:461
  54.2 2.4 slice.409
  58.5 2.5 add_convert_fusion.4
  62.5 1.4 fusion.137
  63.9 1.4 fusion
  66.6 1.6 fusion.82
  68.3 1.9 add_convert_fusion.2.refs_0_
  70.2 23.7 %exchange_forward.3 = (f32[256,768]{1,0:T(8,128)S(1)}, bf16[1024,768]{1,0:T(8,128)(2,1)S(1)}, f32[256,768]{1,0:T(8,128)S(1)}, f32[256,128]{1,0:T(8,128)S(1)}) custom-call(bf16[1024,768]{1,0:T(8,128)(2,1)S(1)} %add_convert_fusion.2.refs_0_, f32[256,768]{1,0:T(8,128)S(1)} %convert_bitcast_fusion.1.refs_1_, f32[1,768]{1,0:T(1,128)S(1)} %get-tuple-element.201.refs_2_, ...), custom_call_target="tpu_custom_call" | custom-call | flops 3932160 | bytes 50000000 | tf_op jit(solution)/shard_map/exchange_forward/pallas_call | solution.py:228
  95.6 10.5 %all-gather.7.cloned.1.call-done = bf16[768,1536]{1,0:T(8,128)(2,1)} async-done(((bf16[96,1536]{1,0:T(8,128)(2,1)}), bf16[768,1536]{1,0:T(8,128)(2,1)}) %all-gather.7.cloned.1.call-update) | async-done | bytes 2359312 | tf_op jit(solution)/shard_map/all_gather | solution.py:473
  106.1 2.8 fusion.100
  109.0 2.1 add_convert_fusion.1.refs_0_
  111.1 24.1 %exchange_forward.4 = (f32[256,768]{1,0:T(8,128)S(1)}, bf16[1024,768]{1,0:T(8,128)(2,1)S(1)}, f32[256,768]{1,0:T(8,128)S(1)}, f32[256,128]{1,0:T(8,128)S(1)}) custom-call(bf16[1024,768]{1,0:T(8,128)(2,1)S(1)} %add_convert_fusion.1.refs_0_, f32[256,768]{1,0:T(8,128)S(1)} %get-tuple-element.48.refs_1_, f32[1,768]{1,0:T(1,128)S(1)} %get-tuple-element.197.refs_2_, ...), custom_call_target="tpu_custom_call" | custom-call | flops 3932160 | bytes 50000000 | tf_op jit(solution)/shard_map/exchange_forward/pallas_call | solution.py:228
  136.1 12.1 %all-gather.9.cloned.1.call-done = bf16[768,768]{1,0:T(8,128)(2,1)} async-done(((bf16[96,768]{1,0:T(8,128)(2,1)}), bf16[768,768]{1,0:T(8,128)(2,1)}) %all-gather.9.cloned.1.call-update) | async-done | bytes 1179664 | tf_op jit(solution)/shard_map/all_gather | solution.py:475
  148.2 2.4 add_convert_fusion.3
  151.8 1.4 fusion.139
  153.7 1.4 fusion.1
  155.8 1.8 fusion.83
  158.3 1.8 add_convert_fusion.refs_0_
  160.1 23.9 %exchange_forward.5 = (f32[256,768]{1,0:T(8,128)S(1)}, bf16[1024,768]{1,0:T(8,128)(2,1)S(1)}, f32[256,768]{1,0:T(8,128)S(1)}, f32[256,128]{1,0:T(8,128)S(1)}) custom-call(bf16[1024,768]{1,0:T(8,128)(2,1)S(1)} %add_convert_fusion.refs_0_, f32[256,768]{1,0:T(8,128)S(1)} %get-tuple-element.50.refs_1_, f32[1,768]{1,0:T(1,128)S(1)} %get-tuple-element.200.refs_2_, ...), custom_call_target="tpu_custom_call" | custom-call | flops 3932160 | bytes 50000000 | tf_op jit(solution)/shard_map/exchange_forward/pallas_call | solution.py:228
  185.2 16.9 %all-gather.11.cloned.1.call-done = bf16[768,1536]{1,0:T(8,128)(2,1)} async-done(((bf16[96,1536]{1,0:T(8,128)(2,1)}), bf16[768,1536]{1,0:T(8,128)(2,1)}) %all-gather.11.cloned.1.call-update) | async-done | bytes 2359312 | tf_op jit(solution)/shard_map/all_gather | solution.py:476
  202.1 3.3 fusion.92
  205.4 2.1 convolution_add_fusion
  207.8 1.6 copy.107
  210.0 14.1 %all-gather.13.cloned.1.call-done = bf16[768,1024]{1,0:T(8,128)(2,1)} async-done(((bf16[192,1024]{1,0:T(8,128)(2,1)}), bf16[768,1024]{1,0:T(8,128)(2,1)}) %all-gather.13.cloned.1.call-update) | async-done | bytes 1572880 | tf_op jit(solution)/shard_map/all_gather | solution.py:516
  225.3 6.7 %convert_reduce_fusion.1 = (f32[768]{0:T(1024)S(1)}, bf16[1024,768]{1,0:T(8,128)(2,1)S(1)}) fusion(bf16[768,1024]{1,0:T(8,128)(2,1)} %all-gather.13.cloned.1.call-done, bf16[768,1536]{1,0:T(8,128)(2,1)} %all-gather.11.cloned.1.call-done, f32[1024,768]{1,0:T(8,128)} %copy-done.94, f32[768]{0:T(1024)S(1)} %reshape.693), kind=kOutput, calls=%fused_computation.46 | convolution fusion | flops 1229192448 | bytes 7477248 | tf_op jit(solution)/shard_map/dot_general | solution.py:554
  232.0 1.4 convolution_convert_fusion.3.refs_0_
  233.5 31.5 %exchange_backward.4 = (f32[256,768]{1,0:T(8,128)S(1)}, bf16[1024,768]{1,0:T(8,128)(2,1)S(1)}, f32[8,768]{1,0:T(8,128)S(1)}) custom-call(bf16[1024,768]{1,0:T(8,128)(2,1)S(1)} %convolution_convert_fusion.3.refs_0_, f32[256,768]{1,0:T(8,128)S(1)} %convert_bitcast_fusion.2.refs_1_, f32[1,768]{1,0:T(1,128)S(1)} %get-tuple-element.200.refs_2_, ...), custom_call_target="tpu_custom_call" | custom-call | flops 3932160 | bytes 50000000 | tf_op jit(solution)/shard_map/exchange_backward/pallas_call | solution.py:228
  267.3 1.8 convolution_convert_fusion.10
  269.1 2.8 multiply_reduce_fusion.3
  274.2 1.5 convolution_convert_fusion.5
  276.5 1.8 convolution_convert_fusion.4
  278.3 1.6 pad_maximum_fusion
  279.9 7.0 %multiply_reduce_fusion.1 = (f32[3,512]{1,0:T(4,128)S(1)}, f32[3,512,1024]{2,1,0:T(8,128)}) fusion(f32[3,512,1024]{2,1,0:T(8,128)} %copy-done.20, f32[3,512]{1,0:T(4,128)S(1)} %log_add_fusion.2, bf16[1024,3,64]{0,2,1:T(8,128)(2,1)} %bitcast.354, bf16[1,1024,3,64]{1,3,2,0:T(8,128)(2,1)} %bitcast.341), kind=kOutput, calls=%fused_computation.4 | convolution fusion | flops 206043648 | bytes 13185024 | tf_op jit(solution)/shard_map/sqhd,skhd->shqk/dot_general | solution.py:717
  287.0 5.5 %multiply_convert_fusion.1 = bf16[3,512,1024]{2,1,0:T(8,128)(2,1)S(1)} fusion(f32[3,512,1024]{2,1,0:T(8,128)} %get-tuple-element.213, f32[3,512,1024]{2,1,0:T(8,128)} %copy-done.20, f32[3,512]{1,0:T(4,128)S(1)} %get-tuple-element.212, f32[3,512]{1,0:T(4,128)S(1)} %log_add_fusion.2), kind=kLoop, calls=%fused_computation.3 | loop fusion | flops 6291456 | bytes 15740928 | tf_op jit(solution)/shard_map/convert_element_type | solution.py:733
  296.2 1.3 convert_reduce_fusion.8
  299.4 1.3 copy.89
  300.7 3.0 convolution_convert_fusion.1.refs_0_
  303.8 2.0 copy.108
  308.1 22.8 %exchange_backward.5 = (f32[256,768]{1,0:T(8,128)S(1)}, bf16[1024,768]{1,0:T(8,128)(2,1)S(1)}, f32[8,768]{1,0:T(8,128)S(1)}) custom-call(bf16[1024,768]{1,0:T(8,128)(2,1)S(1)} %convolution_convert_fusion.1.refs_0_, f32[256,768]{1,0:T(8,128)S(1)} %copy-done.10, f32[1,768]{1,0:T(1,128)S(1)} %get-tuple-element.197.refs_2_, f32[256,768]{1,0:T(8,128)S(1)} %copy-done.6, ...), custom_call_target="tpu_custom_call" | custom-call | flops 3932160 | bytes 50000000 | tf_op jit(solution)/shard_map/exchange_backward/pallas_call | solution.py:228
  330.9 6.4 %convert_reduce_fusion.2 = (f32[768]{0:T(1024)S(1)}, bf16[1024,768]{1,0:T(8,128)(2,1)S(1)}) fusion(bf16[1024,768]{1,0:T(8,128)(2,1)S(1)} %get-tuple-element.62, bf16[768,1536]{1,0:T(8,128)(2,1)S(1)} %copy-done.89, f32[1024,768]{1,0:T(8,128)} %copy-done.92, f32[768]{0:T(1024)S(1)} %reshape.688), kind=kOutput, calls=%fused_computation.47 | convolution fusion | flops 1229192448 | bytes 7478272 | tf_op jit(solution)/shard_map/dot_general | solution.py:554
  337.3 1.4 convolution_convert_fusion.2.refs_0_
  339.0 22.8 %exchange_backward.6 = (f32[256,768]{1,0:T(8,128)S(1)}, bf16[1024,768]{1,0:T(8,128)(2,1)S(1)}, f32[8,768]{1,0:T(8,128)S(1)}) custom-call(bf16[1024,768]{1,0:T(8,128)(2,1)S(1)} %convolution_convert_fusion.2.refs_0_, f32[256,768]{1,0:T(8,128)S(1)} %get-tuple-element.63.refs_1_, f32[1,768]{1,0:T(1,128)S(1)} %get-tuple-element.201.refs_2_, ...), custom_call_target="tpu_custom_call" | custom-call | flops 3932160 | bytes 50000000 | tf_op jit(solution)/shard_map/exchange_backward/pallas_call | solution.py:228
  362.7 1.2 convolution_convert_fusion.12
  363.9 1.9 copy.87
  365.8 4.5 convolution_convert_fusion.7
  370.3 2.7 convolution_convert_fusion.6
  373.0 7.6 %concatenate.90 = bf16[768,2496]{1,0:T(8,128)(2,1)} concatenate(bf16[768,192]{1,0:T(8,128)(2,1)} %copy.87, bf16[768,768]{1,0:T(8,128)(2,1)} %convolution_convert_fusion.7, bf16[768,768]{1,0:T(8,128)(2,1)} %convolution_convert_fusion.6, bf16[768,192]{1,0:T(8,128)(2,1)} %copy.88, bf16[768,576]{1,0:T(8,128)(2,1)} %copy.89), dimensions={1} | concatenate | bytes 7667712 | tf_op jit(solution)/shard_map/concatenate | solution.py:612
  385.5 2.0 copy.92
  387.5 1.6 convert_reduce_fusion.4
  392.6 1.8 convolution_convert_fusion.9
  394.4 2.7 fusion.69
  397.1 5.5 %convert_reduce_fusion.10 = (f32[3,64]{1,0:T(4,128)}, bf16[1,1024,3,64]{1,3,2,0:T(8,128)(2,1)}) fusion(f32[3,512,1024]{2,1,0:T(8,128)} %copy-done.19, f32[3,512]{1,0:T(4,128)S(1)} %log_add_fusion, bf16[1,1024,3,64]{1,3,2,0:T(8,128)(2,1)S(1)} %bitcast.345, f32[1,512,3,64]{1,3,2,0:T(8,128)S(1)} %fusion.69), kind=kOutput, calls=%fused_computation.164 | convolution fusion | flops 205258560 | bytes 7283456 | tf_op jit(solution)/shard_map/shqk,sqhd->skhd/dot_general | solution.py:724
  402.5 1.3 reshape.673
  403.9 1.8 multiply_reduce_fusion.2
  407.7 1.9 multiply_reduce_fusion
  409.5 1.6 multiply_convert_fusion
  413.1 2.2 fusion.72
  416.0 1.5 convolution_convert_fusion.refs_0_
  417.8 23.7 %exchange_backward.7 = (f32[256,768]{1,0:T(8,128)}, bf16[1024,768]{1,0:T(8,128)(2,1)S(1)}, f32[8,768]{1,0:T(8,128)S(1)}) custom-call(bf16[1024,768]{1,0:T(8,128)(2,1)S(1)} %convolution_convert_fusion.refs_0_, f32[256,768]{1,0:T(8,128)S(1)} %copy-done.8, f32[1,768]{1,0:T(1,128)S(1)} %get-tuple-element.196.refs_2_, f32[256,768]{1,0:T(8,128)S(1)} %copy-done.2, ...), custom_call_target="tpu_custom_call" | custom-call | flops 3932160 | bytes 50000000 | tf_op jit(solution)/shard_map/exchange_backward/pallas_call | solution.py:228
  441.8 1.2 copy.93
  444.3 2.6 fusion.106
  446.9 41.5 %row_sum.1 = (f32[96,576]{1,0:T(8,128)S(1)}, f32[16,576]{1,0:T(8,128)S(1)}) custom-call(f32[8,96,576]{2,1,0:T(8,128)S(1)} %bitcast.326, f32[8,16,576]{2,1,0:T(8,128)S(1)} %reshape.682.loose), custom_call_target="tpu_custom_call" | custom-call | bytes 80000000 | tf_op jit(solution)/shard_map/row_sum/pallas_call | solution.py:381
  (374 shorter events, 65.3 us)
Async XLA Ops:
  7.2 7.4 %copy-start.77 = (bf16[2,768]{1,0:T(2,128)(2,1)S(1)}, bf16[2,768]{1,0:T(2,128)(2,1)}, u32[]{:S(2)}) copy-start(bf16[2,768]{1,0:T(2,128)(2,1)} %param.27) | copy-start | bytes 9220
  7.2 7.4 %copy-start.63 = (bf16[2,768]{1,0:T(2,128)(2,1)S(1)}, bf16[2,768]{1,0:T(2,128)(2,1)}, u32[]{:S(2)}) copy-start(bf16[2,768]{1,0:T(2,128)(2,1)} %param.26) | copy-start | bytes 9220
  7.2 8.2 %copy-start.11 = (bf16[192,1024]{1,0:T(8,128)(2,1)S(1)}, bf16[192,1024]{1,0:T(8,128)(2,1)}, u32[]{:S(2)}) copy-start(bf16[192,1024]{1,0:T(8,128)(2,1)} %block.1) | copy-start | bytes 1179652
  7.2 45.8 %all-gather.15.cloned.1.call-start = ((), (), s32[]{:S(2)}) async-start(), calls=%async_computation.9 | async-start | bytes 1548288 | tf_op jit(solution)/shard_map/all_gather | solution.py:461
  10.9 95.3 %all-gather.7.cloned.1.call-start = ((), (), s32[]{:S(2)}) async-start(), calls=%async_computation.3 | async-start | bytes 2654208 | tf_op jit(solution)/shard_map/all_gather | solution.py:473
  12.8 135.4 %all-gather.9.cloned.1.call-start = ((), (), s32[]{:S(2)}) async-start(), calls=%async_computation.4 | async-start | bytes 1327104 | tf_op jit(solution)/shard_map/all_gather | solution.py:475
  13.7 188.4 %all-gather.11.cloned.1.call-start = ((), (), s32[]{:S(2)}) async-start(), calls=%async_computation.5 | async-start | bytes 2654208 | tf_op jit(solution)/shard_map/all_gather | solution.py:476
  14.5 209.6 %all-gather.13.cloned.1.call-start = ((), (), s32[]{:S(2)}) async-start(), calls=%async_computation.6 | async-start | bytes 1966080 | tf_op jit(solution)/shard_map/all_gather | solution.py:516
  14.6 43.9 %copy-start.82 = (f32[768]{0:T(1024)}, f32[768]{0:T(1024)S(1)}, u32[]{:S(2)}) copy-start(f32[768]{0:T(1024)S(1)} %get-tuple-element.234) | copy-start | bytes 9220
  14.6 43.9 %copy-start.84 = (f32[768]{0:T(1024)}, f32[768]{0:T(1024)S(1)}, u32[]{:S(2)}) copy-start(f32[768]{0:T(1024)S(1)} %get-tuple-element.235) | copy-start | bytes 9220
  15.4 13.7 %copy-start.78 = (bf16[2,768]{1,0:T(2,128)(2,1)S(1)}, bf16[2,768]{1,0:T(2,128)(2,1)}, u32[]{:S(2)}) copy-start(bf16[2,768]{1,0:T(2,128)(2,1)} %param.32) | copy-start | bytes 9220
  15.4 13.8 %copy-start.79 = (bf16[2,768]{1,0:T(2,128)(2,1)S(1)}, bf16[2,768]{1,0:T(2,128)(2,1)}, u32[]{:S(2)}) copy-start(bf16[2,768]{1,0:T(2,128)(2,1)} %param.33) | copy-start | bytes 9220
  28.4 30.0 %copy-start = (bf16[768,1024]{1,0:T(8,128)(2,1)}, bf16[768,1024]{1,0:T(8,128)(2,1)S(1)}, u32[]{:S(2)}) copy-start(bf16[768,1024]{1,0:T(8,128)(2,1)S(1)} %first_gather.1) | copy-start | bytes 4718596
  29.6 32.9 %copy-start.32 = (pred[512,1024]{1,0:T(8,128)(4,1)}, pred[512,1024]{1,0:T(8,128)(4,1)S(1)}, u32[]{:S(2)}) copy-start(pred[512,1024]{1,0:T(8,128)(4,1)S(1)} %iota_compare_fusion) | copy-start | bytes 1572868
  29.6 28.9 %copy-start.67 = (f32[1024]{0:T(1024)}, f32[1024]{0:T(1024)S(1)}, u32[]{:S(2)}) copy-start(f32[1024]{0:T(1024)S(1)} %broadcast_multiply_fusion) | copy-start | bytes 12292
  30.1 31.0 %copy-start.86 = (f32[1024]{0:T(1024)}, f32[1024]{0:T(1024)S(1)}, u32[]{:S(2)}) copy-start(f32[1024]{0:T(1024)S(1)} %add_rsqrt_fusion) | copy-start | bytes 12292
  30.4 23.7 %copy-start.80 = (f32[256]{0:T(256)}, f32[256]{0:T(256)S(1)}, u32[]{:S(2)}) copy-start(f32[256]{0:T(256)S(1)} %add_rsqrt_fusion.1) | copy-start | bytes 3076
  61.2 4.8 copy-start.38
  62.0 3.3 copy-start.21
  94.8 14.2 %copy-start.14 = (bf16[1024,768]{1,0:T(8,128)(2,1)}, bf16[1024,768]{1,0:T(8,128)(2,1)S(1)}, u32[]{:S(2)}) copy-start(bf16[1024,768]{1,0:T(8,128)(2,1)S(1)} %get-tuple-element.47) | copy-start | bytes 4718596
  95.4 208.4 %reduce-scatter.10.cloned.1.call-start = ((), (), s32[]{:S(2)}) async-start(), calls=%async_computation.10 | async-start | bytes 1966080
  136.1 14.5 %copy-start.15 = (bf16[1024,768]{1,0:T(8,128)(2,1)}, bf16[1024,768]{1,0:T(8,128)(2,1)S(1)}, u32[]{:S(2)}) copy-start(bf16[1024,768]{1,0:T(8,128)(2,1)S(1)} %get-tuple-element.49) | copy-start | bytes 4718596
  150.7 6.9 %copy-start.40 = (bf16[1024,192]{0,1:T(8,128)(2,1)}, bf16[1024,192]{0,1:T(8,128)(2,1)S(1)}, u32[]{:S(2)}) copy-start(bf16[1024,192]{0,1:T(8,128)(2,1)S(1)} %get-tuple-element.150) | copy-start | bytes 1179652
  151.5 6.1 %copy-start.23 = (f32[3,512,512]{1,2,0:T(8,128)}, f32[3,512,512]{1,2,0:T(8,128)S(1)}, u32[]{:S(2)}) copy-start(f32[3,512,512]{1,2,0:T(8,128)S(1)} %get-tuple-element.211) | copy-start | bytes 9437188
  202.0 3.3 copy-start.90
  209.5 284.3 %reduce-scatter.8.cloned.1.call-start = ((), (), s32[]{:S(2)}) async-start(), calls=%async_computation.8 | async-start | bytes 2654208 | tf_op jit(solution)/shard_map/reduce_scatter | solution.py:408
  225.3 6.7 %copy-start.91 = (bf16[768,1536]{1,0:T(8,128)(2,1)S(1)}, bf16[768,1536]{1,0:T(8,128)(2,1)}, u32[]{:S(2)}) copy-start(bf16[768,1536]{1,0:T(8,128)(2,1)} %all-gather.11.cloned.1.call-done) | copy-start | bytes 7077892
  265.9 3.2 copy-start.41
  269.1 3.0 copy-start.24
  287.0 208.0 %reduce-scatter.6.cloned.1.call-start = ((), (), s32[]{:S(2)}) async-start(), calls=%async_computation.7 | async-start | bytes 4423680 | tf_op jit(solution)/shard_map/reduce_scatter | solution.py:408
  287.0 5.5 %copy-start.31 = (bf16[1024,192]{0,1:T(8,128)(2,1)S(1)}, bf16[1024,192]{0,1:T(8,128)(2,1)}, u32[]{:S(2)}) copy-start(bf16[1024,192]{0,1:T(8,128)(2,1)} %copy-done.29) | copy-start | bytes 1179652
  287.0 6.6 %copy-start.49 = (bf16[1,512,3,64]{1,3,2,0:T(8,128)(2,1)S(1)}, bf16[1,512,3,64]{1,3,2,0:T(8,128)(2,1)}, u32[]{:S(2)}) copy-start(bf16[1,512,3,64]{1,3,2,0:T(8,128)(2,1)} %fusion.77) | copy-start | bytes 589828
  287.0 6.8 %copy-start.45 = (bf16[1024,192]{0,1:T(8,128)(2,1)S(1)}, bf16[1024,192]{0,1:T(8,128)(2,1)}, u32[]{:S(2)}) copy-start(bf16[1024,192]{0,1:T(8,128)(2,1)} %copy-done.44) | copy-start | bytes 1179652
  287.0 7.4 %copy-start.25 = (f32[3,512,512]{1,2,0:T(8,128)S(1)}, f32[3,512,512]{1,2,0:T(8,128)}, u32[]{:S(2)}) copy-start(f32[3,512,512]{1,2,0:T(8,128)} %copy-done.23) | copy-start | bytes 9437188
  292.6 3.2 slice-start.2
  293.8 3.7 copy-start.55
  308.1 22.8 %copy-start.89 = (bf16[768,1536]{1,0:T(8,128)(2,1)S(1)}, bf16[768,1536]{1,0:T(8,128)(2,1)}, u32[]{:S(2)}) copy-start(bf16[768,1536]{1,0:T(8,128)(2,1)} %all-gather.7.cloned.1.call-done) | copy-start | bytes 7077892
  330.9 6.4 %copy-start.12 = (bf16[1024,768]{1,0:T(8,128)(2,1)}, bf16[1024,768]{1,0:T(8,128)(2,1)S(1)}, u32[]{:S(2)}) copy-start(bf16[1024,768]{1,0:T(8,128)(2,1)S(1)} %get-tuple-element.62) | copy-start | bytes 4718596
  338.7 24.0 %copy-start.48 = (bf16[1,1024,3,64]{1,3,2,0:T(8,128)(2,1)S(1)}, bf16[1,1024,3,64]{1,3,2,0:T(8,128)(2,1)}, u32[]{:S(2)}) copy-start(bf16[1,1024,3,64]{1,3,2,0:T(8,128)(2,1)} %copy-done.47) | copy-start | bytes 1179652
  365.8 4.5 copy-start.13
  365.8 4.5 copy-start.93
  380.7 13.7 %copy-start.61 = (f32[3,512]{1,0:T(4,128)}, f32[3,512]{1,0:T(4,128)S(1)}, u32[]{:S(2)}) copy-start(f32[3,512]{1,0:T(4,128)S(1)} %log_add_fusion.1) | copy-start | bytes 18436
  394.4 8.2 %copy-start.36 = (bf16[1024,192]{0,1:T(8,128)(2,1)}, bf16[1024,192]{0,1:T(8,128)(2,1)S(1)}, u32[]{:S(2)}) copy-start(bf16[1024,192]{0,1:T(8,128)(2,1)S(1)} %convolution_convert_fusion.9) | copy-start | bytes 1179652
  397.1 6.8 %copy-start.22 = (f32[3,512,512]{1,2,0:T(8,128)S(1)}, f32[3,512,512]{1,2,0:T(8,128)}, u32[]{:S(2)}) copy-start(f32[3,512,512]{1,2,0:T(8,128)} %copy-done.21) | copy-start | bytes 9437188
  397.1 6.8 %copy-start.39 = (bf16[1024,192]{0,1:T(8,128)(2,1)S(1)}, bf16[1024,192]{0,1:T(8,128)(2,1)}, u32[]{:S(2)}) copy-start(bf16[1024,192]{0,1:T(8,128)(2,1)} %copy-done.38) | copy-start | bytes 1179652
  403.8 3.2 slice-start
  417.7 25.4 %copy-start.64 = (f32[2,768]{1,0:T(2,128)S(1)}, f32[2,768]{1,0:T(2,128)}, u32[]{:S(2)}) copy-start(f32[2,768]{1,0:T(2,128)} %slice.370) | copy-start | bytes 18436
  417.7 25.4 %copy-start.65 = (f32[2,768]{1,0:T(2,128)S(1)}, f32[2,768]{1,0:T(2,128)}, u32[]{:S(2)}) copy-start(f32[2,768]{1,0:T(2,128)} %slice.369) | copy-start | bytes 18436
  417.7 25.4 %copy-start.66 = (f32[2,768]{1,0:T(2,128)S(1)}, f32[2,768]{1,0:T(2,128)}, u32[]{:S(2)}) copy-start(f32[2,768]{1,0:T(2,128)} %slice.368) | copy-start | bytes 18436
  417.7 26.2 %copy-start.69 = (f32[8,24]{1,0:T(8,128)S(1)}, f32[8,24]{1,0:T(8,128)}, u32[]{:S(2)}) copy-start(f32[8,24]{1,0:T(8,128)} %reshape.679) | copy-start | bytes 2308
  417.7 26.2 %copy-start.70 = (f32[8,24]{1,0:T(8,128)S(1)}, f32[8,24]{1,0:T(8,128)}, u32[]{:S(2)}) copy-start(f32[8,24]{1,0:T(8,128)} %reshape.676) | copy-start | bytes 2308
  417.7 26.2 %copy-start.71 = (f32[8,24]{1,0:T(8,128)S(1)}, f32[8,24]{1,0:T(8,128)}, u32[]{:S(2)}) copy-start(f32[8,24]{1,0:T(8,128)} %reshape.674) | copy-start | bytes 2308
  417.7 26.2 %copy-start.72 = (f32[8,96]{1,0:T(8,128)S(1)}, f32[8,96]{1,0:T(8,128)}, u32[]{:S(2)}) copy-start(f32[8,96]{1,0:T(8,128)} %reshape.680) | copy-start | bytes 9220
  417.7 26.2 %copy-start.73 = (f32[8,24]{1,0:T(8,128)S(1)}, f32[8,24]{1,0:T(8,128)}, u32[]{:S(2)}) copy-start(f32[8,24]{1,0:T(8,128)} %reshape.678) | copy-start | bytes 2308
  417.7 26.2 %copy-start.74 = (f32[8,24]{1,0:T(8,128)S(1)}, f32[8,24]{1,0:T(8,128)}, u32[]{:S(2)}) copy-start(f32[8,24]{1,0:T(8,128)} %reshape.677) | copy-start | bytes 2308
  417.7 26.2 %copy-start.75 = (f32[8,96]{1,0:T(8,128)S(1)}, f32[8,96]{1,0:T(8,128)}, u32[]{:S(2)}) copy-start(f32[8,96]{1,0:T(8,128)} %reshape.675) | copy-start | bytes 9220
  417.8 26.2 %copy-start.76 = (f32[8,24]{1,0:T(8,128)S(1)}, f32[8,24]{1,0:T(8,128)}, u32[]{:S(2)}) copy-start(f32[8,24]{1,0:T(8,128)} %reshape.673) | copy-start | bytes 2308
  417.8 26.4 %copy-start.1 = (bf16[768,1024]{1,0:T(8,128)(2,1)S(1)}, bf16[768,1024]{1,0:T(8,128)(2,1)}, u32[]{:S(2)}) copy-start(bf16[768,1024]{1,0:T(8,128)(2,1)} %copy-done) | copy-start | bytes 4718596
  417.8 26.4 %copy-start.51 = (bf16[1,1024,3,64]{1,3,2,0:T(8,128)(2,1)S(1)}, bf16[1,1024,3,64]{1,3,2,0:T(8,128)(2,1)}, u32[]{:S(2)}) copy-start(bf16[1,1024,3,64]{1,3,2,0:T(8,128)(2,1)} %get-tuple-element.221) | copy-start | bytes 1179652
  417.8 26.4 %copy-start.54 = (bf16[1,1024,3,64]{1,3,2,0:T(8,128)(2,1)S(1)}, bf16[1,1024,3,64]{1,3,2,0:T(8,128)(2,1)}, u32[]{:S(2)}) copy-start(bf16[1,1024,3,64]{1,3,2,0:T(8,128)(2,1)} %get-tuple-element.147) | copy-start | bytes 1179652
  417.8 26.4 %copy-start.68 = (f32[1024]{0:T(1024)S(1)}, f32[1024]{0:T(1024)}, u32[]{:S(2)}) copy-start(f32[1024]{0:T(1024)} %copy-done.67) | copy-start | bytes 12292
  417.8 26.4 %copy-start.83 = (f32[768]{0:T(1024)S(1)}, f32[768]{0:T(1024)}, u32[]{:S(2)}) copy-start(f32[768]{0:T(1024)} %copy-done.82) | copy-start | bytes 9220
  417.8 26.4 %copy-start.85 = (f32[768]{0:T(1024)S(1)}, f32[768]{0:T(1024)}, u32[]{:S(2)}) copy-start(f32[768]{0:T(1024)} %copy-done.84) | copy-start | bytes 9220
  417.8 26.4 %copy-start.87 = (f32[1024]{0:T(1024)S(1)}, f32[1024]{0:T(1024)}, u32[]{:S(2)}) copy-start(f32[1024]{0:T(1024)} %copy-done.86) | copy-start | bytes 12292
  (47 other events, 85.7 us)
Sparse Core Ops, SparseCore 0:
  11.0 41.9 all-gather.14
  55.8 50.3 all-gather.6
  108.9 39.2 all-gather.8
  150.8 51.1 all-gather.10
  203.5 20.5 all-gather.12
  226.5 36.6 reduce-scatter.9
  287.1 66.0 reduce-scatter.7
  380.8 100.7 reduce-scatter.5
